TPU v7x, 32 devices: a whole 2x2x4 slice. The times are simulated.
32 devices in a mesh: groups: 2 (over x), req: 8 (over z, y), head: 2 (over core).
Axes of the slice: x: 2, y: 2, z: 4, core: 2. Of those that a mesh axis runs over, the one named last changes fastest.
Arguments:
- queries: bfloat16 [2048, 32, 128], P(('groups', 'req'), 'head'), parts along dimension 0, may hold values from -100 to 100
- new_keys: bfloat16 [2048, 2, 128], P(('groups', 'req'), 'head'), parts along dimension 0, may hold values from -4.5 to 4.5
- new_values: bfloat16 [2048, 2, 128], P(('groups', 'req'), 'head'), parts along dimension 0, may hold values from -6 to 6
- cluster_kv: bfloat16 [1024, 2, 2, 128, 128], P(('groups', 'req'), 'head'), parts along dimension 0, may hold values from -6 to 6
- cluster_len: int32 [32], P('groups'), parts along dimension 0, may hold values from 1 to 4096, 40960 in all
- piece_slot: int32 [32, 32], P('groups'), parts along dimension 0, may hold values from 0 to 511, as said below
- cluster_ids: int32 [16, 2, 2], P('groups', 'head'), parts along dimension 0, may hold values from 0 to 15, all different within a row
- w_out: bfloat16 [4096, 4096], P('head', 'req'), may hold values from -0.09375 to 0.09375
Outputs:
- projected: bfloat16 [2048, 4096], P(('groups', 'req', 'head')), parts along dimension 0
There are 2 independent parts, one for each index of `groups`. A program takes and returns all parts, laid end to end along the dimension named above; an argument that names none is the same for every part. Nothing has to cross between parts.
Inputs may be any that keep to these rules, and one draw needn't show every extreme that they name: `cluster_ids`: for each request and KV head, 2 distinct cluster numbers. A permutation of the slots: piece p of cluster c lies in slot piece_slot[c, p], stored on index slot // 64 of req, and every cluster has exactly 4 of its pieces on every index of req.
All inputs are finite; a program needn't handle non-finite values.
Results may differ from a plain program's by a relative error of at most 0.0052.
Values may be sent and summed in bfloat16 or wider, within the bound.
No kernel may reach another device: no remote copies, remote signals or barrier semaphores. Data moves between devices by JAX's collectives and lax.ppermute only.
A program may use at most 128 MiB of HBM per device.

v0:
```python
import functools
import math

import jax
import jax.numpy as jnp
from jax import lax
from jax.experimental import pallas as pl
from jax.experimental.pallas import tpu as pltpu
from jax.sharding import PartitionSpec as P

LOW = -1e30
VMEM_SMALL = 16 * 1024 * 1024
VMEM_MOST = 60 * 1024 * 1024
COST = pl.CostEstimate(flops=1024, bytes_accessed=1024, transcendentals=0)
SHORT = pl.CostEstimate(flops=1 << 31, bytes_accessed=1024, transcendentals=0)
LONG = pl.CostEstimate(flops=1 << 40, bytes_accessed=1024, transcendentals=0)


def swap(array, axis, size, mask):
    return lax.ppermute(array, axis, [(i, i ^ mask) for i in range(size)])


def pack_kernel(wanted, per_peer, slot_ref, ids_ref, kv_ref, *rest):
    outs, (slots, ids, table, sems, first) = rest[:-5], rest[-5:]
    loads = [
        pltpu.make_async_copy(slot_ref, slots, first.at[0]),
        pltpu.make_async_copy(ids_ref, ids, first.at[1]),
    ]
    for copy in loads:
        copy.start()
    for copy in loads:
        copy.wait()
    me = lax.axis_index("req")
    pieces = slots.shape[1]
    held = kv_ref.shape[0]
    picks = ids.shape[0]
    low = me * held
    copies = []
    for out, mask in zip(outs, wanted):
        for s in range(picks):
            row = (len(copies) // per_peer) % table.shape[0]
            c = ids[s, me ^ mask]

            def scan(p, count, c=c, row=row):
                slot = slots[c, p] - low
                table[row, count] = slot
                return count + ((slot >= 0) & (slot < held)).astype(jnp.int32)

            lax.fori_loop(0, pieces, scan, jnp.int32(0), unroll=8)
            for k in range(per_peer):
                copies.append(
                    pltpu.make_async_copy(kv_ref.at[table[row, k], 0], out.at[s * per_peer + k], sems.at[len(copies)])
                )
                copies[-1].start()
    for copy in copies:
        copy.wait()


def pack(piece_slot, plan, cluster_kv, wanted, per_peer):
    count = plan.shape[0] * per_peer
    shape = jax.ShapeDtypeStruct((count,) + cluster_kv.shape[2:], cluster_kv.dtype)
    hbm = pl.BlockSpec(memory_space=pltpu.HBM)
    total = len(wanted)
    return pl.pallas_call(
        functools.partial(pack_kernel, wanted, per_peer),
        out_shape=[shape] * total,
        in_specs=[hbm] * 3,
        out_specs=[pl.BlockSpec(memory_space=pltpu.VMEM)] * total,
        scratch_shapes=[
            pltpu.SMEM(piece_slot.shape, jnp.int32),
            pltpu.SMEM(plan.shape, jnp.int32),
            pltpu.SMEM((total * plan.shape[0], per_peer + 1), jnp.int32),
            pltpu.SemaphoreType.DMA((total * count,)),
            pltpu.SemaphoreType.DMA((2,)),
        ],
        compiler_params=pltpu.CompilerParams(vmem_limit_bytes=VMEM_MOST),
        cost_estimate=COST,
        name="pack_pieces",
    )(piece_slot, plan, cluster_kv)


def fold(values, keys, op):
    parts = [values[:, i * keys : (i + 1) * keys] for i in range(values.shape[1] // keys)]
    while len(parts) > 1:
        parts = [op(parts[i], parts[i + 1]) if i + 1 < len(parts) else parts[i] for i in range(0, len(parts), 2)]
    return parts[0]


def to_lines(column, eye):
    keys = eye.shape[0]
    return jnp.concatenate(
        [
            jnp.sum(jnp.where(eye, column[n : n + keys], 0.0), axis=0, keepdims=True)
            for n in range(0, column.shape[0], keys)
        ],
        axis=0,
    )


def to_column(lines, eye):
    return jnp.concatenate(
        [jnp.sum(jnp.where(eye, lines[n : n + 1], 0.0), axis=1, keepdims=True) for n in range(lines.shape[0])],
        axis=0,
    )


def diagonal(keys):
    return lax.broadcasted_iota(jnp.int32, (keys, keys), 0) == lax.broadcasted_iota(jnp.int32, (keys, keys), 1)


def attend_kernel(settings, *refs):
    own, heads, rows_step, sources, scale, mode, earlier = settings
    refs = list(refs)

    def take(n):
        taken, refs[:] = refs[:n], refs[n:]
        return taken

    q_ref, valid_ref = take(2)
    own_k, own_v = take(2) if own else (None, None)
    got = take(len(sources))
    before = take(2) if earlier else None
    outs = take(2)
    scores, own_scores, tops, lse = refs
    rows, size = q_ref.shape
    each, _, keys, _ = got[0].shape
    lines = rows // keys
    group = rows_step // keys
    steps = rows // rows_step
    lane = lax.broadcasted_iota(jnp.int32, (1, keys), 1)
    eye = diagonal(keys)
    biases, any_valid = [], jnp.int32(0)
    for j in sources:
        valid = [valid_ref[j, e] for e in range(each)]
        biases.append(jnp.concatenate([jnp.where(lane < v, 0.0, LOW) for v in valid], axis=1))
        any_valid = sum(valid, any_valid)

    def dot_t(x, y):
        return lax.dot_general(x, y, (((1,), (1,)), ((), ())), preferred_element_type=jnp.float32)

    def score(i, turn):
        q = q_ref[pl.ds(pl.multiple_of(i * rows_step, rows_step), rows_step), :]
        found = []
        if own:
            s = dot_t(q, own_k[...])
            position = (lax.broadcasted_iota(jnp.int32, s.shape, 0) + i * rows_step) // heads
            s = jnp.where(position >= lax.broadcasted_iota(jnp.int32, s.shape, 1), s * scale, LOW)
            own_scores[turn] = s
            found.append(s)
        for b, pieces in enumerate(got):
            s = dot_t(q, pieces[:, 0].reshape(each * keys, size)) * scale + biases[b]
            scores[turn, b] = s
            found.append(fold(s, keys, jnp.maximum))
        tops[turn] = functools.reduce(jnp.maximum, found)

    def weigh(i, turn):
        here = pl.ds(pl.multiple_of(i * rows_step, rows_step), rows_step)
        top = jnp.max(tops[turn], axis=1, keepdims=True)
        total, mix = [], []
        if own:
            p = jnp.exp2(own_scores[turn] - top)
            total.append(fold(p, keys, jnp.add))
            mix.append(jnp.dot(p.astype(jnp.bfloat16), own_v[...], preferred_element_type=jnp.float32))
        for b, pieces in enumerate(got):
            p = jnp.exp2(scores[turn, b] - top)
            total.append(fold(p, keys, jnp.add))
            values = pieces[:, 1].reshape(each * keys, size)
            mix.append(jnp.dot(p.astype(jnp.bfloat16), values, preferred_element_type=jnp.float32))
        total = jnp.sum(functools.reduce(jnp.add, total), axis=1, keepdims=True)
        normal = functools.reduce(jnp.add, mix) / total
        mine = to_lines(top + jnp.log2(total), eye)
        if not own:
            mine = jnp.where(any_valid > 0, mine, LOW)
        if earlier:
            old, logs = before[0][here, :], before[1][i]
            peak = jnp.maximum(logs, mine)
            power = jnp.exp2(logs - peak)
            whole = power + jnp.exp2(mine - peak)
            normal = normal + to_column(power / whole, eye) * (old - normal)
            mine = peak + jnp.log2(whole)
        if mode == "state":
            outs[0][here, :] = normal
            outs[1][i] = mine
        else:
            lse[i] = mine
            low = normal.astype(jnp.bfloat16)
            for n in range(2):

                @pl.when(i // (steps // 2) == n)
                def _(n=n):
                    spot = pl.multiple_of((i - n * (steps // 2)) * rows_step, rows_step)
                    outs[n][pl.ds(spot, rows_step), :] = low

    score(0, 0)

    def each_step(i, carry):
        for turn in range(2):
            score(jnp.minimum(2 * i + turn + 1, steps - 1), 1 - turn)
            weigh(2 * i + turn, turn)
        return carry

    lax.fori_loop(0, steps // 2, each_step, 0)
    if mode == "packed":
        left = jnp.concatenate([lse[i] for i in range(steps)], axis=0)
        for n in range(3):
            part = left.astype(jnp.bfloat16)
            outs[0][pl.ds(rows // 2 + n * lines, lines), :] = part
            left = left - part.astype(jnp.float32)


def attend(name, mode, heads, q, valid, got, own=None, earlier=None, cost=COST):
    rows, size = q.shape
    sources = list(got)
    each, _, keys, _ = got[sources[0]].shape
    rows_step = math.gcd(rows, 512)
    lines = rows // keys
    scale = size ** -0.5 * math.log2(math.e)
    settings = (own is not None, heads, rows_step, sources, scale, mode, earlier is not None)
    smem = pl.BlockSpec(memory_space=pltpu.SMEM)
    vmem = pl.BlockSpec(memory_space=pltpu.VMEM)
    operands = [q, valid] + list(own or ()) + list(got.values()) + list(earlier or ())
    if mode == "state":
        out_shape = [
            jax.ShapeDtypeStruct((rows, size), jnp.float32),
            jax.ShapeDtypeStruct((rows // rows_step, rows_step // keys, keys), jnp.float32),
        ]
    else:
        out_shape = [jax.ShapeDtypeStruct((n, size), jnp.bfloat16) for n in (rows // 2 + 3 * lines, rows // 2)]
    limit = min(VMEM_MOST, VMEM_SMALL + 8 * len(sources) * rows_step * each * keys)
    return pl.pallas_call(
        functools.partial(attend_kernel, settings),
        out_shape=out_shape,
        in_specs=[vmem, smem] + [vmem] * (len(operands) - 2),
        out_specs=[vmem] * len(out_shape),
        scratch_shapes=[
            pltpu.VMEM((2, len(sources), rows_step, each * keys), jnp.float32),
            pltpu.VMEM((2, rows_step if own is not None else 8, own[0].shape[0] if own else keys), jnp.float32),
            pltpu.VMEM((2, rows_step, keys), jnp.float32),
            pltpu.VMEM((rows // rows_step, rows_step // keys, keys), jnp.float32),
        ],
        compiler_params=pltpu.CompilerParams(vmem_limit_bytes=limit),
        cost_estimate=cost,
        name=name,
    )(*operands)


def combine_kernel(heads, out_mine, lse_mine, other, more, attended, scratch):
    rows, size = out_mine.shape
    steps, group, keys = lse_mine.shape
    lines = steps * group
    eye = diagonal(keys)
    mine = jnp.concatenate([lse_mine[i] for i in range(steps)], axis=0)
    theirs = sum(other[pl.ds(rows // 2 + n * lines, lines), :].astype(jnp.float32) for n in range(3))
    top = jnp.maximum(mine, theirs)
    mine, theirs = jnp.exp2(mine - top), jnp.exp2(theirs - top)
    share = theirs / (mine + theirs)
    for n in range(lines):
        here = pl.ds(n * keys, keys)
        a = out_mine[here, :]
        b = other[here, :] if n < lines // 2 else more[pl.ds((n - lines // 2) * keys, keys), :]
        scratch[here, :] = a + to_column(share[n : n + 1], eye) * (b.astype(jnp.float32) - a)
    tokens = rows // heads
    for h in range(heads):
        attended[:, h * size : (h + 1) * size] = scratch[pl.ds(h, tokens, stride=heads), :].astype(attended.dtype)


def combine(state, parts, heads):
    rows, size = state[0].shape
    vmem = pl.BlockSpec(memory_space=pltpu.VMEM)
    return pl.pallas_call(
        functools.partial(combine_kernel, heads),
        out_shape=jax.ShapeDtypeStruct((rows // heads, heads * size), jnp.bfloat16),
        in_specs=[vmem] * 4,
        out_specs=vmem,
        scratch_shapes=[pltpu.VMEM((rows, size), jnp.float32)],
        compiler_params=pltpu.CompilerParams(vmem_limit_bytes=VMEM_SMALL),
        cost_estimate=LONG,
        name="combine",
    )(*state, *parts)


def project_kernel(attended, w_mine, w_sooner, w_later, away, keep, scratch):
    core = lax.axis_index("head")
    share = away.shape[1]
    cut = w_sooner.shape[0]

    def dot(x, w):
        return jnp.dot(x, w[...], preferred_element_type=jnp.float32)

    scratch[0] = dot(attended[...], w_mine)
    scratch[1] = dot(attended[:, :cut], w_sooner) + dot(attended[:, cut:], w_later)
    for side in range(2):
        away[side] = scratch[side, pl.ds(pl.multiple_of((core ^ 1) * share, share), share), :].astype(jnp.bfloat16)
        keep[side] = scratch[side, pl.ds(pl.multiple_of(core * share, share), share), :]


def project(attended, w_mine, w_sooner, w_later, cores):
    tokens, depth = attended.shape
    width = w_mine.shape[1]
    share = tokens // cores
    vmem = pl.BlockSpec(memory_space=pltpu.VMEM)
    return pl.pallas_call(
        project_kernel,
        out_shape=[
            jax.ShapeDtypeStruct((2, share, width), jnp.bfloat16),
            jax.ShapeDtypeStruct((2, share, width), jnp.float32),
        ],
        in_specs=[vmem] * 4,
        out_specs=[vmem] * 2,
        scratch_shapes=[pltpu.VMEM((2, tokens, width), jnp.float32)],
        compiler_params=pltpu.CompilerParams(vmem_limit_bytes=VMEM_SMALL),
        cost_estimate=COST,
        name="project",
    )(attended, w_mine, w_sooner, w_later)


def place_kernel(masks, *refs):
    parts, out = refs[:-1], refs[-1]
    me = lax.axis_index("req")
    width = parts[0].shape[2]
    for part, mask in zip(parts, masks):
        for side in range(2):
            column = ((me ^ mask) ^ side) * width
            out[:, pl.ds(pl.multiple_of(column, width), width)] = part[side]


def place(parts, masks):
    _, rows, width = parts[0].shape
    vmem = pl.BlockSpec(memory_space=pltpu.VMEM)
    return pl.pallas_call(
        functools.partial(place_kernel, masks),
        out_shape=jax.ShapeDtypeStruct((rows, 2 * len(parts) * width), parts[0].dtype),
        in_specs=[vmem] * len(parts),
        out_specs=vmem,
        compiler_params=pltpu.CompilerParams(vmem_limit_bytes=VMEM_SMALL),
        cost_estimate=COST,
        name="place_columns",
    )(*parts)


def after(value, *others):
    return lax.optimization_barrier((value, others))[0]


def local(queries, new_keys, new_values, cluster_kv, cluster_len, piece_slot, cluster_ids, w_out):
    me = lax.axis_index("req")
    peers = lax.axis_size("req")
    cores = lax.axis_size("head")
    tokens, heads, size = queries.shape
    held = cluster_kv.shape[0]
    keys = cluster_kv.shape[3]
    pieces = piece_slot.shape[1]
    per_peer = pieces // peers
    half = peers // 2
    masks = list(range(1, half))
    last, late, early = masks[-1:], masks[-2:-1], masks[:-2]

    plan = cluster_ids[:, 0]
    first = pack(piece_slot, plan.T, cluster_kv, [m ^ half for m in masks], per_peer)
    got = {m: swap(a, "req", peers, m) for a, m in zip(first, masks)}
    q_mine = queries.reshape(tokens * heads, size)
    q_theirs = swap(q_mine, "req", peers, half)
    second = pack(piece_slot, plan.T, after(cluster_kv, *first), [half, 0] + masks, per_peer)
    got[0], own_pieces, second = second[0], second[1], dict(zip(masks, second[2:]))

    owner = piece_slot // held
    position = jnp.arange(pieces, dtype=jnp.int32)
    same = (owner[:, :, None] == owner[:, None, :]) & (position[:, None] > position[None, :])[None]
    rank = jnp.sum(same.astype(jnp.int32), axis=2)

    def table(request):
        chosen = lax.dynamic_index_in_dim(plan, request, 0, keepdims=False)
        sender = me ^ jnp.arange(half, dtype=jnp.int32)
        fits = (owner[chosen][None, :, None, :] == sender[:, None, None, None]) & (
            rank[chosen][None, :, None, :] == jnp.arange(per_peer, dtype=jnp.int32)[None, None, :, None]
        )
        filled = jnp.clip(cluster_len[chosen][:, None] - position[None, :] * keys, 0, keys)
        return jnp.sum(jnp.where(fits, filled[None, :, None, :], 0), axis=3).reshape(half, -1)

    valid_theirs, valid_mine = table(me ^ half), table(me)

    def some(chosen):
        return {m: got[m] for m in chosen}

    own = attend(
        "attend_own_local", "state", heads, q_mine, valid_mine, {0: own_pieces}, (new_keys[:, 0], new_values[:, 0])
    )
    q_theirs = after(q_theirs, *own)
    state = attend("attend_partner_local", "state", heads, q_theirs, valid_theirs, some([0]), cost=SHORT)
    if early:
        state = attend("attend_partner_early", "state", heads, q_theirs, valid_theirs, some(early), earlier=state)
    got_mine = {m: swap(after(second[m], *state), "req", peers, m) for m in masks}
    state = attend("attend_partner_late", "state", heads, q_theirs, valid_theirs, some(late), earlier=state)
    part = attend("attend_partner_last", "packed", heads, q_theirs, valid_theirs, some(last), earlier=state)
    got = got_mine
    cut = w_out.shape[0] * 3 // 16
    w_sooner = swap(after(w_out[:cut], *part), "req", peers, 1)
    own = after(own, *part)
    part = [swap(a, "req", peers, half) for a in part]

    if early:
        own = attend("attend_own_early", "state", heads, q_mine, valid_mine, some(early), earlier=own)
    own = after(own, w_sooner)
    own = attend("attend_own_late", "state", heads, q_mine, valid_mine, some(late), earlier=own)
    w_later = swap(after(w_out[cut:], *own), "req", peers, 1)
    own = attend("attend_own_last", "state", heads, q_mine, valid_mine, some(last), earlier=own)
    attended = combine(own, part, heads)

    have = {0: attended}
    bit = half
    while bit > 1:
        for mask in list(have):
            rows = after(have[mask], have[bit]) if mask else attended
            have[mask ^ bit] = swap(rows, "req", peers, bit)
        bit //= 2

    single = [m for m in have if m and not m & (m - 1)]
    results, last = {}, ()
    for mask in sorted(have, key=lambda m: (m not in single + [0], -m)):
        if mask in single + [0]:
            rows = after(have[mask], *[have[m] for m in single])
        else:
            rows = after(have[mask], *last, *[results[m] for m in single if m != half])
        away, keep = last = project(rows, w_out, w_sooner, w_later, cores)
        away = swap(away, "head", cores, 1)
        summed = (keep + away.astype(jnp.float32)).astype(jnp.bfloat16)
        results[mask] = swap(summed, "req", peers, mask) if mask else summed
    return place(list(results.values()), list(results))


def solution(mesh):
    return jax.shard_map(
        local,
        mesh=mesh,
        in_specs=(
            P(("groups", "req"), "head", None),
            P(("groups", "req"), "head", None),
            P(("groups", "req"), "head", None),
            P(("groups", "req"), "head", None, None, None),
            P("groups"),
            P("groups", None),
            P("groups", "head", None),
            P("head", "req"),
        ),
        out_specs=P(("groups", "req", "head"), None),
        check_vma=False,
    )
```

profile of v0, /device:TPU:0, one launch (start us, length us, event | category | flops | bytes accessed | tf_op | source)
XLA Modules:
  0.0 141.5 jit_solution(809065102987432317)
XLA Ops:
  0.0 4.0 %collective-permute-start = (bf16[2048,128]{1,0:T(8,128)(2,1)}, bf16[2048,128]{1,0:T(8,128)(2,1)S(1)}, u32[]{:S(2)}, u32[]{:S(2)}) collective-permute-start(bf16[2048,128]{1,0:T(8,128)(2,1)} %bitcast.14), channel_id=1, source_target_pairs={{0,8},{2,10},{4,12},{6,14},{8,0},{10,2},{12,4},{14,6},{1,9},{3,11}... | collective-permute-start | bytes 1572872 | tf_op jit(solution)/shard_map/ppermute | solution.py:20
  4.0 4.5 %pack_pieces.2 = (bf16[8,2,128,128]{3,2,1,0:T(8,128)(2,1)}, bf16[8,2,128,128]{3,2,1,0:T(8,128)(2,1)}, bf16[8,2,128,128]{3,2,1,0:T(8,128)(2,1)}) custom-call(s32[16,32]{1,0:T(8,128)} %slot_ref.3, s32[2,8]{1,0:T(2,128)} %bitcast.21, bf16[64,1,2,128,128]{4,3,2,1,0:T(8,128)(2,1)} %kv_ref.2), custom_call_target="tpu_custom_call" | custom-call | flops 1024 | bytes 1024 | tf_op jit(solution)/shard_map/pack_pieces/pallas_call | solution.py:64
  8.6 1.6 %collective-permute-start.1 = (bf16[8,2,128,128]{3,2,1,0:T(8,128)(2,1)}, bf16[8,2,128,128]{3,2,1,0:T(8,128)(2,1)}, u32[]{:S(2)}, u32[]{:S(2)}) collective-permute-start(bf16[8,2,128,128]{3,2,1,0:T(8,128)(2,1)} %get-tuple-element.53), channel_id=1, source_target_pairs={{0,2},{2,0},{4,6},{6,4},{8,10},{10,8},{12,14},{14,12},{1,3},{3,1},... | collective-permute-start | bytes 1572872 | tf_op jit(solution)/shard_map/ppermute | solution.py:20
  10.2 1.6 %collective-permute-start.6 = (bf16[8,2,128,128]{3,2,1,0:T(8,128)(2,1)}, bf16[8,2,128,128]{3,2,1,0:T(8,128)(2,1)S(1)}, u32[]{:S(2)}, u32[]{:S(2)}) collective-permute-start(bf16[8,2,128,128]{3,2,1,0:T(8,128)(2,1)} %get-tuple-element.54), channel_id=1, source_target_pairs={{0,4},{2,6},{4,0},{6,2},{8,12},{10,14},{12,8},{14,10},{1,5},{3,7},... | collective-permute-start | bytes 1572872 | tf_op jit(solution)/shard_map/ppermute | solution.py:20
  11.7 0.4 collective-permute-start.5
  12.2 0.2 dynamic-slice_reduce_fusion
  12.4 0.6 gather_fusion
  13.0 0.6 gather_fusion.3
  13.6 0.6 gather_fusion.2
  14.2 0.6 gather_fusion.5
  14.8 0.5 convert_reduce_fusion
  15.3 0.6 gather_fusion.1
  15.9 0.1 broadcast_compare_fusion
  15.9 0.1 subtract_clamp_fusion
  16.0 0.0 copy-start.2
  16.0 0.0 copy-start.6
  16.1 5.8 %pack_pieces.3 = (bf16[8,2,128,128]{3,2,1,0:T(8,128)(2,1)}, bf16[8,2,128,128]{3,2,1,0:T(8,128)(2,1)}, bf16[8,2,128,128]{3,2,1,0:T(8,128)(2,1)}, bf16[8,2,128,128]{3,2,1,0:T(8,128)(2,1)}, bf16[8,2,128,128]{3,2,1,0:T(8,128)(2,1)}) custom-call(s32[16,32]{1,0:T(8,128)} %slot_ref.3, s32[2,8]{1,0:T(2,128)} %bitcast.22, bf16[64,1,2,128,128]{4,3,2,1,0:T(8,128)(2,1)} %kv_ref.2), custom_call_target="tpu_custom_call" | custom-call | flops 1024 | bytes 1024 | tf_op jit(solution)/shard_map/pack_pieces/pallas_call | solution.py:64
  21.8 0.2 select_reduce_fusion.1
  22.1 0.1 reshape.175.refs_1_
  22.2 1.0 copy-done.5
  23.2 5.3 %attend_own_local.1 = (f32[2048,128]{1,0:T(8,128)S(1)}, f32[4,4,128]{2,1,0:T(4,128)S(1)}) custom-call(bf16[2048,128]{1,0:T(8,128)(2,1)S(1)} %bitcast.15, s32[4,8]{1,0:T(4,128)S(1)} %reshape.175.refs_1_, bf16[128,128]{1,0:T(8,128)(2,1)S(1)} %bitcast.19, bf16[128,128]{1,0:T(8,128)(2,1)S(1)} %bitcast.20, bf16[8,2,128,128]{3,2,1,0:T(8,128)(2,1)S(1)} %copy-done.5), custom_call_target="tpu_custom_call" | custom-call | flops 1024 | bytes 1024 | tf_op jit(solution)/shard_map/attend_own_local/pallas_call | solution.py:230
  28.5 0.6 gather_fusion.4
  29.1 0.2 select_reduce_fusion
  29.3 0.1 reshape.176.refs_1_
  29.4 1.0 copy-done.8
  30.5 4.1 %attend_partner_local.1 = (f32[2048,128]{1,0:T(8,128)S(1)}, f32[4,4,128]{2,1,0:T(4,128)S(1)}) custom-call(bf16[2048,128]{1,0:T(8,128)(2,1)S(1)} %collective-permute-done.refs_0_, s32[4,8]{1,0:T(4,128)S(1)} %reshape.176.refs_1_, bf16[8,2,128,128]{3,2,1,0:T(8,128)(2,1)S(1)} %copy-done.8), custom_call_target="tpu_custom_call" | custom-call | flops 2147483648 | bytes 1024 | tf_op jit(solution)/shard_map/attend_partner_local/pallas_call | solution.py:230
  34.6 5.1 %attend_partner_early.1 = (f32[2048,128]{1,0:T(8,128)S(1)}, f32[4,4,128]{2,1,0:T(4,128)S(1)}) custom-call(bf16[2048,128]{1,0:T(8,128)(2,1)S(1)} %collective-permute-done.refs_0_, s32[4,8]{1,0:T(4,128)S(1)} %reshape.176.refs_1_, bf16[8,2,128,128]{3,2,1,0:T(8,128)(2,1)} %collective-permute-done.1.refs_2_, f32[2048,128]{1,0:T(8,128)S(1)} %get-tuple-element.63.refs_3_, ...), custom_call_target="tpu_custom_call" | custom-call | flops 1024 | bytes 1024 | tf_op jit(solution)/shard_map/attend_partner_early/pallas_call | solution.py:230
  39.8 1.6 %collective-permute-start.4 = (bf16[8,2,128,128]{3,2,1,0:T(8,128)(2,1)S(1)}, bf16[8,2,128,128]{3,2,1,0:T(8,128)(2,1)S(1)}, u32[]{:S(2)}, u32[]{:S(2)}) collective-permute-start(bf16[8,2,128,128]{3,2,1,0:T(8,128)(2,1)S(1)} %copy-done.13), channel_id=1, source_target_pairs={{0,2},{2,0},{4,6},{6,4},{8,10},{10,8},{12,14},{14,12},{1,3},{3,1},... | collective-permute-start | bytes 1572872 | tf_op jit(solution)/shard_map/ppermute | solution.py:20
  41.4 1.6 %collective-permute-start.3 = (bf16[8,2,128,128]{3,2,1,0:T(8,128)(2,1)S(1)}, bf16[8,2,128,128]{3,2,1,0:T(8,128)(2,1)S(1)}, u32[]{:S(2)}, u32[]{:S(2)}) collective-permute-start(bf16[8,2,128,128]{3,2,1,0:T(8,128)(2,1)S(1)} %copy-done.12), channel_id=1, source_target_pairs={{0,4},{2,6},{4,0},{6,2},{8,12},{10,14},{12,8},{14,10},{1,5},{3,7},... | collective-permute-start | bytes 1572872 | tf_op jit(solution)/shard_map/ppermute | solution.py:20
  42.9 0.4 collective-permute-start.2
  43.4 4.6 %attend_partner_late.1 = (f32[2048,128]{1,0:T(8,128)S(1)}, f32[4,4,128]{2,1,0:T(4,128)S(1)}) custom-call(bf16[2048,128]{1,0:T(8,128)(2,1)S(1)} %collective-permute-done.refs_0_, s32[4,8]{1,0:T(4,128)S(1)} %reshape.176.refs_1_, bf16[8,2,128,128]{3,2,1,0:T(8,128)(2,1)S(1)} %collective-permute-done.6.refs_2_, f32[2048,128]{1,0:T(8,128)S(1)} %get-tuple-element.65.refs_3_, ...), custom_call_target="tpu_custom_call" | custom-call | flops 1024 | bytes 1024 | tf_op jit(solution)/shard_map/attend_partner_late/pallas_call | solution.py:230
  47.9 5.1 %attend_partner_last.1 = (bf16[1072,128]{1,0:T(8,128)(2,1)S(1)}, bf16[1024,128]{1,0:T(8,128)(2,1)S(1)}) custom-call(bf16[2048,128]{1,0:T(8,128)(2,1)S(1)} %collective-permute-done.refs_0_, s32[4,8]{1,0:T(4,128)S(1)} %reshape.176.refs_1_, bf16[8,2,128,128]{3,2,1,0:T(8,128)(2,1)S(1)} %collective-permute-done.5.refs_2_, ...), custom_call_target="tpu_custom_call" | custom-call | flops 1024 | bytes 1024 | tf_op jit(solution)/shard_map/attend_partner_last/pallas_call | solution.py:230
  53.0 1.6 %collective-permute-start.7 = (bf16[384,512]{1,0:T(8,128)(2,1)S(1)}, bf16[384,512]{1,0:T(8,128)(2,1)S(1)}, u32[]{:S(2)}, u32[]{:S(2)}) collective-permute-start(bf16[384,512]{1,0:T(8,128)(2,1)S(1)} %slice.6), channel_id=1, source_target_pairs={{0,2},{2,0},{4,6},{6,4},{8,10},{10,8},{12,14},{14,12},{1,3},{3,1},... | collective-permute-start | bytes 1179656 | tf_op jit(solution)/shard_map/ppermute | solution.py:20
  54.6 0.3 collective-permute-start.8
  54.9 2.0 %collective-permute-done.4.refs_2_ = bf16[8,2,128,128]{3,2,1,0:T(8,128)(2,1)S(1)} collective-permute-done((bf16[8,2,128,128]{3,2,1,0:T(8,128)(2,1)S(1)}, bf16[8,2,128,128]{3,2,1,0:T(8,128)(2,1)S(1)}, u32[]{:S(2)}, u32[]{:S(2)}) %collective-permute-start.4) | collective-permute-done | bytes 524320 | tf_op jit(solution)/shard_map/ppermute | solution.py:20
  56.9 0.6 collective-permute-start.9
  57.5 1.3 slice.7
  58.9 4.6 %attend_own_early.1 = (f32[2048,128]{1,0:T(8,128)S(1)}, f32[4,4,128]{2,1,0:T(4,128)S(1)}) custom-call(bf16[2048,128]{1,0:T(8,128)(2,1)S(1)} %bitcast.16, s32[4,8]{1,0:T(4,128)S(1)} %reshape.175.refs_1_, bf16[8,2,128,128]{3,2,1,0:T(8,128)(2,1)S(1)} %collective-permute-done.4.refs_2_, f32[2048,128]{1,0:T(8,128)S(1)} %get-tuple-element.76.refs_3_, ...), custom_call_target="tpu_custom_call" | custom-call | flops 1024 | bytes 1024 | tf_op jit(solution)/shard_map/attend_own_early/pallas_call | solution.py:230
  63.4 2.0 %collective-permute-done.7.w_sooner = bf16[384,512]{1,0:T(8,128)(2,1)S(1)} collective-permute-done((bf16[384,512]{1,0:T(8,128)(2,1)S(1)}, bf16[384,512]{1,0:T(8,128)(2,1)S(1)}, u32[]{:S(2)}, u32[]{:S(2)}) %collective-permute-start.7) | collective-permute-done | bytes 393248 | tf_op jit(solution)/shard_map/ppermute | solution.py:20
  65.5 2.4 %collective-permute-done.3.refs_2_ = bf16[8,2,128,128]{3,2,1,0:T(8,128)(2,1)S(1)} collective-permute-done((bf16[8,2,128,128]{3,2,1,0:T(8,128)(2,1)S(1)}, bf16[8,2,128,128]{3,2,1,0:T(8,128)(2,1)S(1)}, u32[]{:S(2)}, u32[]{:S(2)}) %collective-permute-start.3) | collective-permute-done | bytes 524320 | tf_op jit(solution)/shard_map/ppermute | solution.py:20
  67.8 4.6 %attend_own_late.1 = (f32[2048,128]{1,0:T(8,128)S(1)}, f32[4,4,128]{2,1,0:T(4,128)S(1)}) custom-call(bf16[2048,128]{1,0:T(8,128)(2,1)S(1)} %bitcast.17, s32[4,8]{1,0:T(4,128)S(1)} %reshape.175.refs_1_, bf16[8,2,128,128]{3,2,1,0:T(8,128)(2,1)S(1)} %collective-permute-done.3.refs_2_, f32[2048,128]{1,0:T(8,128)S(1)} %get-tuple-element.81.refs_3_, ...), custom_call_target="tpu_custom_call" | custom-call | flops 1024 | bytes 1024 | tf_op jit(solution)/shard_map/attend_own_late/pallas_call | solution.py:230
  72.4 0.6 collective-permute-start.12
  73.0 4.4 %collective-permute-done.2.refs_2_ = bf16[8,2,128,128]{3,2,1,0:T(8,128)(2,1)S(1)} collective-permute-done((bf16[8,2,128,128]{3,2,1,0:T(8,128)(2,1)S(1)}, bf16[8,2,128,128]{3,2,1,0:T(8,128)(2,1)S(1)}, u32[]{:S(2)}, u32[]{:S(2)}) %collective-permute-start.2) | collective-permute-done | bytes 524320 | tf_op jit(solution)/shard_map/ppermute | solution.py:20
  77.4 4.8 %attend_own_last.1 = (f32[2048,128]{1,0:T(8,128)S(1)}, f32[4,4,128]{2,1,0:T(4,128)S(1)}) custom-call(bf16[2048,128]{1,0:T(8,128)(2,1)S(1)} %bitcast.18, s32[4,8]{1,0:T(4,128)S(1)} %reshape.175.refs_1_, bf16[8,2,128,128]{3,2,1,0:T(8,128)(2,1)S(1)} %collective-permute-done.2.refs_2_, f32[2048,128]{1,0:T(8,128)S(1)} %get-tuple-element.83.refs_3_, ...), custom_call_target="tpu_custom_call" | custom-call | flops 1024 | bytes 1024 | tf_op jit(solution)/shard_map/attend_own_last/pallas_call | solution.py:230
  82.2 0.6 combine.1.attended
  82.8 3.2 %collective-permute-start.10 = (bf16[128,2048]{1,0:T(8,128)(2,1)S(1)}, bf16[128,2048]{1,0:T(8,128)(2,1)S(1)}, u32[]{:S(2)}, u32[]{:S(2)}) collective-permute-start(bf16[128,2048]{1,0:T(8,128)(2,1)S(1)} %combine.1.attended), channel_id=1, source_target_pairs={{0,8},{2,10},{4,12},{6,14},{8,0},{10,2},{12,4},{14,6},{1,9},{3,11}... | collective-permute-start | bytes 1572872 | tf_op jit(solution)/shard_map/ppermute | solution.py:20
  86.0 22.5 %collective-permute-done.10.attended = bf16[128,2048]{1,0:T(8,128)(2,1)S(1)} collective-permute-done((bf16[128,2048]{1,0:T(8,128)(2,1)S(1)}, bf16[128,2048]{1,0:T(8,128)(2,1)S(1)}, u32[]{:S(2)}, u32[]{:S(2)}) %collective-permute-start.10) | collective-permute-done | bytes 524320 | tf_op jit(solution)/shard_map/ppermute | solution.py:20
  108.5 0.5 collective-permute-done.11.attended
  109.0 1.2 collective-permute-start.18
  110.2 3.8 %collective-permute-done.12.w_later = bf16[1664,512]{1,0:T(8,128)(2,1)} collective-permute-done((bf16[1664,512]{1,0:T(8,128)(2,1)}, bf16[1664,512]{1,0:T(8,128)(2,1)}, u32[]{:S(2)}, u32[]{:S(2)}) %collective-permute-start.12) | collective-permute-done | bytes 1703968 | tf_op jit(solution)/shard_map/ppermute | solution.py:20
  113.9 2.3 %project.5 = (bf16[2,64,512]{2,1,0:T(8,128)(2,1)S(1)}, f32[2,64,512]{2,1,0:T(8,128)S(1)}) custom-call(bf16[128,2048]{1,0:T(8,128)(2,1)S(1)} %collective-permute-done.11.attended, bf16[2048,512]{1,0:T(8,128)(2,1)S(1)} %copy-done.1, bf16[384,512]{1,0:T(8,128)(2,1)S(1)} %copy-done.4, bf16[1664,512]{1,0:T(8,128)(2,1)} %collective-permute-done.12.w_later), custom_call_target="tpu_custom_call" | custom-call | flops 1024 | bytes 1024 | tf_op jit(solution)/shard_map/project/pallas_call | solution.py:302
  116.2 0.1 collective-permute-start.15
  116.3 1.3 collective-permute-done.15
  117.7 2.6 %collective-permute-start.16 = (bf16[2,64,512]{2,1,0:T(8,128)(2,1)S(1)}, bf16[2,64,512]{2,1,0:T(8,128)(2,1)S(1)}, u32[]{:S(2)}, u32[]{:S(2)}) collective-permute-start(bf16[2,64,512]{2,1,0:T(8,128)(2,1)S(1)} %add_convert_fusion.2), channel_id=1, source_target_pairs={{0,4},{2,6},{4,0},{6,2},{8,12},{10,14},{12,8},{14,10},{1,5},{3,7},... | collective-permute-start | bytes 393224 | tf_op jit(solution)/shard_map/ppermute | solution.py:20
  120.2 2.3 %project.4 = (bf16[2,64,512]{2,1,0:T(8,128)(2,1)S(1)}, f32[2,64,512]{2,1,0:T(8,128)S(1)}) custom-call(bf16[128,2048]{1,0:T(8,128)(2,1)S(1)} %collective-permute-done.10.attended, bf16[2048,512]{1,0:T(8,128)(2,1)S(1)} %copy-done.1, bf16[384,512]{1,0:T(8,128)(2,1)S(1)} %copy-done.4, bf16[1664,512]{1,0:T(8,128)(2,1)} %collective-permute-done.12.w_later), custom_call_target="tpu_custom_call" | custom-call | flops 1024 | bytes 1024 | tf_op jit(solution)/shard_map/project/pallas_call | solution.py:302
  122.5 0.1 collective-permute-start.13
  122.6 2.3 %project.6 = (bf16[2,64,512]{2,1,0:T(8,128)(2,1)S(1)}, f32[2,64,512]{2,1,0:T(8,128)S(1)}) custom-call(bf16[128,2048]{1,0:T(8,128)(2,1)S(1)} %combine.1.attended, bf16[2048,512]{1,0:T(8,128)(2,1)S(1)} %copy-done.1, bf16[384,512]{1,0:T(8,128)(2,1)S(1)} %copy-done.4, bf16[1664,512]{1,0:T(8,128)(2,1)} %collective-permute-done.12.w_later), custom_call_target="tpu_custom_call" | custom-call | flops 1024 | bytes 1024 | tf_op jit(solution)/shard_map/project/pallas_call | solution.py:302
  124.9 0.6 collective-permute-start.17
  125.4 2.3 %project.7 = (bf16[2,64,512]{2,1,0:T(8,128)(2,1)S(1)}, f32[2,64,512]{2,1,0:T(8,128)S(1)}) custom-call(bf16[128,2048]{1,0:T(8,128)(2,1)S(1)} %collective-permute-done.18.attended, bf16[2048,512]{1,0:T(8,128)(2,1)S(1)} %copy-done.1, bf16[384,512]{1,0:T(8,128)(2,1)S(1)} %copy-done.4, bf16[1664,512]{1,0:T(8,128)(2,1)} %collective-permute-done.12.w_later), custom_call_target="tpu_custom_call" | custom-call | flops 1024 | bytes 1024 | tf_op jit(solution)/shard_map/project/pallas_call | solution.py:302
  127.7 0.1 collective-permute-start.19
  127.8 1.9 %collective-permute-start.14 = (bf16[2,64,512]{2,1,0:T(8,128)(2,1)S(1)}, bf16[2,64,512]{2,1,0:T(8,128)(2,1)S(1)}, u32[]{:S(2)}, u32[]{:S(2)}) collective-permute-start(bf16[2,64,512]{2,1,0:T(8,128)(2,1)S(1)} %add_convert_fusion.3), channel_id=1, source_target_pairs={{0,8},{2,10},{4,12},{6,14},{8,0},{10,2},{12,4},{14,6},{1,9},{3,11}... | collective-permute-start | bytes 393224 | tf_op jit(solution)/shard_map/ppermute | solution.py:20
  129.8 2.4 %collective-permute-start.20 = (bf16[2,64,512]{2,1,0:T(8,128)(2,1)S(1)}, bf16[2,64,512]{2,1,0:T(8,128)(2,1)S(1)}, u32[]{:S(2)}, u32[]{:S(2)}) collective-permute-start(bf16[2,64,512]{2,1,0:T(8,128)(2,1)S(1)} %add_convert_fusion), channel_id=1, source_target_pairs={{0,12},{2,14},{4,8},{6,10},{8,4},{10,6},{12,0},{14,2},{1,13},{3,15... | collective-permute-start | bytes 393224 | tf_op jit(solution)/shard_map/ppermute | solution.py:20
  132.2 8.4 %collective-permute-done.14.refs_0_ = bf16[2,64,512]{2,1,0:T(8,128)(2,1)S(1)} collective-permute-done((bf16[2,64,512]{2,1,0:T(8,128)(2,1)S(1)}, bf16[2,64,512]{2,1,0:T(8,128)(2,1)S(1)}, u32[]{:S(2)}, u32[]{:S(2)}) %collective-permute-start.14) | collective-permute-done | bytes 131104 | tf_op jit(solution)/shard_map/ppermute | solution.py:20
  140.7 0.8 place_columns.1
  (51 shorter events, 0.3 us)
Async XLA Ops:
  0.0 13.6 %copy-start = (s32[16]{0:T(128)S(1)}, s32[16]{0:T(128)}, u32[]{:S(2)}) copy-start(s32[16]{0:T(128)} %param.12) | copy-start | bytes 196
  0.0 29.4 %collective-permute-start = (bf16[2048,128]{1,0:T(8,128)(2,1)}, bf16[2048,128]{1,0:T(8,128)(2,1)S(1)}, u32[]{:S(2)}, u32[]{:S(2)}) collective-permute-start(bf16[2048,128]{1,0:T(8,128)(2,1)} %bitcast.14), channel_id=1, source_target_pairs={{0,8},{2,10},{4,12},{6,14},{8,0},{10,2},{12,4},{14,6},{1,9},{3,11}... | collective-permute-start | bytes 1572872 | tf_op jit(solution)/shard_map/ppermute | solution.py:20
  4.0 8.1 %copy-start.9 = (s32[16,32]{1,0:T(8,128)S(1)}, s32[16,32]{1,0:T(8,128)}, u32[]{:S(2)}) copy-start(s32[16,32]{1,0:T(8,128)} %slot_ref.3) | copy-start | bytes 6148
  4.0 8.1 %copy-start.10 = (s32[8,1,2]{0,2,1:T(2,128)S(1)}, s32[8,1,2]{0,2,1:T(2,128)}, u32[]{:S(2)}) copy-start(s32[8,1,2]{0,2,1:T(2,128)} %param.14) | copy-start | bytes 196
  8.6 26.0 %collective-permute-start.1 = (bf16[8,2,128,128]{3,2,1,0:T(8,128)(2,1)}, bf16[8,2,128,128]{3,2,1,0:T(8,128)(2,1)}, u32[]{:S(2)}, u32[]{:S(2)}) collective-permute-start(bf16[8,2,128,128]{3,2,1,0:T(8,128)(2,1)} %get-tuple-element.53), channel_id=1, source_target_pairs={{0,2},{2,0},{4,6},{6,4},{8,10},{10,8},{12,14},{14,12},{1,3},{3,1},... | collective-permute-start | bytes 1572872 | tf_op jit(solution)/shard_map/ppermute | solution.py:20
  10.2 33.2 %collective-permute-start.6 = (bf16[8,2,128,128]{3,2,1,0:T(8,128)(2,1)}, bf16[8,2,128,128]{3,2,1,0:T(8,128)(2,1)S(1)}, u32[]{:S(2)}, u32[]{:S(2)}) collective-permute-start(bf16[8,2,128,128]{3,2,1,0:T(8,128)(2,1)} %get-tuple-element.54), channel_id=1, source_target_pairs={{0,4},{2,6},{4,0},{6,2},{8,12},{10,14},{12,8},{14,10},{1,5},{3,7},... | collective-permute-start | bytes 1572872 | tf_op jit(solution)/shard_map/ppermute | solution.py:20
  11.7 36.2 %collective-permute-start.5 = (bf16[8,2,128,128]{3,2,1,0:T(8,128)(2,1)}, bf16[8,2,128,128]{3,2,1,0:T(8,128)(2,1)S(1)}, u32[]{:S(2)}, u32[]{:S(2)}) collective-permute-start(bf16[8,2,128,128]{3,2,1,0:T(8,128)(2,1)} %get-tuple-element.55), channel_id=1, source_target_pairs={{0,6},{2,4},{4,2},{6,0},{8,14},{10,12},{12,10},{14,8},{1,7},{3,5},... | collective-permute-start | bytes 1572872 | tf_op jit(solution)/shard_map/ppermute | solution.py:20
  16.0 6.1 %copy-start.2 = (bf16[128,16,128]{2,1,0:T(8,128)(2,1)S(1)}, bf16[128,16,128]{2,1,0:T(8,128)(2,1)}, u32[]{:S(2)}) copy-start(bf16[128,16,128]{2,1,0:T(8,128)(2,1)} %param.8) | copy-start | bytes 1572868
  16.0 6.1 %copy-start.6 = (bf16[128,1,128]{2,0,1:T(8,128)(2,1)S(1)}, bf16[128,1,128]{2,0,1:T(8,128)(2,1)}, u32[]{:S(2)}) copy-start(bf16[128,1,128]{2,0,1:T(8,128)(2,1)} %param.9) | copy-start | bytes 98308
  16.1 6.1 %copy-start.7 = (bf16[128,1,128]{2,0,1:T(8,128)(2,1)S(1)}, bf16[128,1,128]{2,0,1:T(8,128)(2,1)}, u32[]{:S(2)}) copy-start(bf16[128,1,128]{2,0,1:T(8,128)(2,1)} %param.10) | copy-start | bytes 98308
  22.2 1.0 copy-start.5
  29.4 1.0 copy-start.8
  30.5 9.3 %copy-start.13 = (bf16[8,2,128,128]{3,2,1,0:T(8,128)(2,1)S(1)}, bf16[8,2,128,128]{3,2,1,0:T(8,128)(2,1)}, u32[]{:S(2)}) copy-start(bf16[8,2,128,128]{3,2,1,0:T(8,128)(2,1)} %get-tuple-element.71) | copy-start | bytes 1572868
  30.5 10.9 %copy-start.12 = (bf16[8,2,128,128]{3,2,1,0:T(8,128)(2,1)S(1)}, bf16[8,2,128,128]{3,2,1,0:T(8,128)(2,1)}, u32[]{:S(2)}) copy-start(bf16[8,2,128,128]{3,2,1,0:T(8,128)(2,1)} %get-tuple-element.69) | copy-start | bytes 1572868
  30.5 12.5 %copy-start.11 = (bf16[8,2,128,128]{3,2,1,0:T(8,128)(2,1)S(1)}, bf16[8,2,128,128]{3,2,1,0:T(8,128)(2,1)}, u32[]{:S(2)}) copy-start(bf16[8,2,128,128]{3,2,1,0:T(8,128)(2,1)} %get-tuple-element.67) | copy-start | bytes 1572868
  34.6 8.7 %copy-start.1 = (bf16[2048,512]{1,0:T(8,128)(2,1)S(1)}, bf16[2048,512]{1,0:T(8,128)(2,1)}, u32[]{:S(2)}) copy-start(bf16[2048,512]{1,0:T(8,128)(2,1)} %w_mine.7) | copy-start | bytes 6291460
  39.8 17.2 %collective-permute-start.4 = (bf16[8,2,128,128]{3,2,1,0:T(8,128)(2,1)S(1)}, bf16[8,2,128,128]{3,2,1,0:T(8,128)(2,1)S(1)}, u32[]{:S(2)}, u32[]{:S(2)}) collective-permute-start(bf16[8,2,128,128]{3,2,1,0:T(8,128)(2,1)S(1)} %copy-done.13), channel_id=1, source_target_pairs={{0,2},{2,0},{4,6},{6,4},{8,10},{10,8},{12,14},{14,12},{1,3},{3,1},... | collective-permute-start | bytes 1572872 | tf_op jit(solution)/shard_map/ppermute | solution.py:20
  41.4 26.4 %collective-permute-start.3 = (bf16[8,2,128,128]{3,2,1,0:T(8,128)(2,1)S(1)}, bf16[8,2,128,128]{3,2,1,0:T(8,128)(2,1)S(1)}, u32[]{:S(2)}, u32[]{:S(2)}) collective-permute-start(bf16[8,2,128,128]{3,2,1,0:T(8,128)(2,1)S(1)} %copy-done.12), channel_id=1, source_target_pairs={{0,4},{2,6},{4,0},{6,2},{8,12},{10,14},{12,8},{14,10},{1,5},{3,7},... | collective-permute-start | bytes 1572872 | tf_op jit(solution)/shard_map/ppermute | solution.py:20
  42.9 34.5 %collective-permute-start.2 = (bf16[8,2,128,128]{3,2,1,0:T(8,128)(2,1)S(1)}, bf16[8,2,128,128]{3,2,1,0:T(8,128)(2,1)S(1)}, u32[]{:S(2)}, u32[]{:S(2)}) collective-permute-start(bf16[8,2,128,128]{3,2,1,0:T(8,128)(2,1)S(1)} %copy-done.11), channel_id=1, source_target_pairs={{0,6},{2,4},{4,2},{6,0},{8,14},{10,12},{12,10},{14,8},{1,7},{3,5},... | collective-permute-start | bytes 1572872 | tf_op jit(solution)/shard_map/ppermute | solution.py:20
  53.0 12.4 %collective-permute-start.7 = (bf16[384,512]{1,0:T(8,128)(2,1)S(1)}, bf16[384,512]{1,0:T(8,128)(2,1)S(1)}, u32[]{:S(2)}, u32[]{:S(2)}) collective-permute-start(bf16[384,512]{1,0:T(8,128)(2,1)S(1)} %slice.6), channel_id=1, source_target_pairs={{0,2},{2,0},{4,6},{6,4},{8,10},{10,8},{12,14},{14,12},{1,3},{3,1},... | collective-permute-start | bytes 1179656 | tf_op jit(solution)/shard_map/ppermute | solution.py:20
  54.6 27.6 %collective-permute-start.8 = (bf16[1072,128]{1,0:T(8,128)(2,1)S(1)}, bf16[1072,128]{1,0:T(8,128)(2,1)S(1)}, u32[]{:S(2)}, u32[]{:S(2)}) collective-permute-start(bf16[1072,128]{1,0:T(8,128)(2,1)S(1)} %get-tuple-element.74), channel_id=1, source_target_pairs={{0,8},{2,10},{4,12},{6,14},{8,0},{10,2},{12,4},{14,6},{1,9},{3,11}... | collective-permute-start | bytes 823304 | tf_op jit(solution)/shard_map/ppermute | solution.py:20
  56.9 25.3 %collective-permute-start.9 = (bf16[1024,128]{1,0:T(8,128)(2,1)S(1)}, bf16[1024,128]{1,0:T(8,128)(2,1)S(1)}, u32[]{:S(2)}, u32[]{:S(2)}) collective-permute-start(bf16[1024,128]{1,0:T(8,128)(2,1)S(1)} %get-tuple-element.75), channel_id=1, source_target_pairs={{0,8},{2,10},{4,12},{6,14},{8,0},{10,2},{12,4},{14,6},{1,9},{3,11}... | collective-permute-start | bytes 786440 | tf_op jit(solution)/shard_map/ppermute | solution.py:20
  65.5 16.7 %copy-start.3 = (bf16[384,512]{1,0:T(8,128)(2,1)}, bf16[384,512]{1,0:T(8,128)(2,1)S(1)}, u32[]{:S(2)}) copy-start(bf16[384,512]{1,0:T(8,128)(2,1)S(1)} %collective-permute-done.7.w_sooner) | copy-start | bytes 1179652
  72.4 41.5 %collective-permute-start.12 = (bf16[1664,512]{1,0:T(8,128)(2,1)}, bf16[1664,512]{1,0:T(8,128)(2,1)}, u32[]{:S(2)}, u32[]{:S(2)}) collective-permute-start(bf16[1664,512]{1,0:T(8,128)(2,1)} %slice.7), channel_id=1, source_target_pairs={{0,2},{2,0},{4,6},{6,4},{8,10},{10,8},{12,14},{14,12},{1,3},{3,1},... | collective-permute-start | bytes 5111816 | tf_op jit(solution)/shard_map/ppermute | solution.py:20
  82.2 31.7 %copy-start.4 = (bf16[384,512]{1,0:T(8,128)(2,1)S(1)}, bf16[384,512]{1,0:T(8,128)(2,1)}, u32[]{:S(2)}) copy-start(bf16[384,512]{1,0:T(8,128)(2,1)} %copy-done.3) | copy-start | bytes 1179652
  82.8 25.7 %collective-permute-start.10 = (bf16[128,2048]{1,0:T(8,128)(2,1)S(1)}, bf16[128,2048]{1,0:T(8,128)(2,1)S(1)}, u32[]{:S(2)}, u32[]{:S(2)}) collective-permute-start(bf16[128,2048]{1,0:T(8,128)(2,1)S(1)} %combine.1.attended), channel_id=1, source_target_pairs={{0,8},{2,10},{4,12},{6,14},{8,0},{10,2},{12,4},{14,6},{1,9},{3,11}... | collective-permute-start | bytes 1572872 | tf_op jit(solution)/shard_map/ppermute | solution.py:20
  86.0 23.0 %collective-permute-start.11 = (bf16[128,2048]{1,0:T(8,128)(2,1)S(1)}, bf16[128,2048]{1,0:T(8,128)(2,1)S(1)}, u32[]{:S(2)}, u32[]{:S(2)}) collective-permute-start(bf16[128,2048]{1,0:T(8,128)(2,1)S(1)} %combine.1.attended), channel_id=1, source_target_pairs={{0,4},{2,6},{4,0},{6,2},{8,12},{10,14},{12,8},{14,10},{1,5},{3,7},... | collective-permute-start | bytes 1572872 | tf_op jit(solution)/shard_map/ppermute | solution.py:20
  109.0 16.4 %collective-permute-start.18 = (bf16[128,2048]{1,0:T(8,128)(2,1)S(1)}, bf16[128,2048]{1,0:T(8,128)(2,1)S(1)}, u32[]{:S(2)}, u32[]{:S(2)}) collective-permute-start(bf16[128,2048]{1,0:T(8,128)(2,1)S(1)} %collective-permute-done.10.attended), channel_id=1, source_target_pairs={{0,4},{2,6},{4,0},{6,2},{8,12},{10,14},{12,8},{14,10},{1,5},{3,7},... | collective-permute-start | bytes 1572872 | tf_op jit(solution)/shard_map/ppermute | solution.py:20
  116.2 1.4 collective-permute-start.15
  117.7 7.8 %collective-permute-start.16 = (bf16[2,64,512]{2,1,0:T(8,128)(2,1)S(1)}, bf16[2,64,512]{2,1,0:T(8,128)(2,1)S(1)}, u32[]{:S(2)}, u32[]{:S(2)}) collective-permute-start(bf16[2,64,512]{2,1,0:T(8,128)(2,1)S(1)} %add_convert_fusion.2), channel_id=1, source_target_pairs={{0,4},{2,6},{4,0},{6,2},{8,12},{10,14},{12,8},{14,10},{1,5},{3,7},... | collective-permute-start | bytes 393224 | tf_op jit(solution)/shard_map/ppermute | solution.py:20
  122.5 5.3 %collective-permute-start.13 = (bf16[2,64,512]{2,1,0:T(8,128)(2,1)S(1)}, bf16[2,64,512]{2,1,0:T(8,128)(2,1)S(1)}, u32[]{:S(2)}, u32[]{:S(2)}) collective-permute-start(bf16[2,64,512]{2,1,0:T(8,128)(2,1)S(1)} %get-tuple-element.90), channel_id=1, source_target_pairs={{0,1},{1,0},{2,3},{3,2},{4,5},{5,4},{6,7},{7,6},{8,9},{9,8},{10,11... | collective-permute-start | bytes 393224 | tf_op jit(solution)/shard_map/ppermute | solution.py:20
  124.9 7.4 %collective-permute-start.17 = (bf16[2,64,512]{2,1,0:T(8,128)(2,1)S(1)}, bf16[2,64,512]{2,1,0:T(8,128)(2,1)S(1)}, u32[]{:S(2)}, u32[]{:S(2)}) collective-permute-start(bf16[2,64,512]{2,1,0:T(8,128)(2,1)S(1)} %get-tuple-element.96), channel_id=1, source_target_pairs={{0,1},{1,0},{2,3},{3,2},{4,5},{5,4},{6,7},{7,6},{8,9},{9,8},{10,11... | collective-permute-start | bytes 393224 | tf_op jit(solution)/shard_map/ppermute | solution.py:20
  127.7 2.1 %collective-permute-start.19 = (bf16[2,64,512]{2,1,0:T(8,128)(2,1)S(1)}, bf16[2,64,512]{2,1,0:T(8,128)(2,1)S(1)}, u32[]{:S(2)}, u32[]{:S(2)}) collective-permute-start(bf16[2,64,512]{2,1,0:T(8,128)(2,1)S(1)} %get-tuple-element.100), channel_id=1, source_target_pairs={{0,1},{1,0},{2,3},{3,2},{4,5},{5,4},{6,7},{7,6},{8,9},{9,8},{10,11... | collective-permute-start | bytes 393224 | tf_op jit(solution)/shard_map/ppermute | solution.py:20
  127.8 12.8 %collective-permute-start.14 = (bf16[2,64,512]{2,1,0:T(8,128)(2,1)S(1)}, bf16[2,64,512]{2,1,0:T(8,128)(2,1)S(1)}, u32[]{:S(2)}, u32[]{:S(2)}) collective-permute-start(bf16[2,64,512]{2,1,0:T(8,128)(2,1)S(1)} %add_convert_fusion.3), channel_id=1, source_target_pairs={{0,8},{2,10},{4,12},{6,14},{8,0},{10,2},{12,4},{14,6},{1,9},{3,11}... | collective-permute-start | bytes 393224 | tf_op jit(solution)/shard_map/ppermute | solution.py:20
  129.8 10.9 %collective-permute-start.20 = (bf16[2,64,512]{2,1,0:T(8,128)(2,1)S(1)}, bf16[2,64,512]{2,1,0:T(8,128)(2,1)S(1)}, u32[]{:S(2)}, u32[]{:S(2)}) collective-permute-start(bf16[2,64,512]{2,1,0:T(8,128)(2,1)S(1)} %add_convert_fusion), channel_id=1, source_target_pairs={{0,12},{2,14},{4,8},{6,10},{8,4},{10,6},{12,0},{14,2},{1,13},{3,15... | collective-permute-start | bytes 393224 | tf_op jit(solution)/shard_map/ppermute | solution.py:20
where the time goes:
time: 143 us; the launch traced here: 142 us
  Pallas kernels  58.8 us (41%)
  waiting for transfers between devices  47.3 us (33%)
  starting transfers between devices  26.4 us (18%)
  local copies, waits for them, and re-layouts  7.4 us (5%)
    ppermute x21, waiting for transfers between devices, swap(): return lax.ppermute(array, axis, [(i, i ^ mask) for i in range(size)])  47.3 us
    pallas_call x8, Pallas kernels, attend(): pl.pallas_call(functools.partial(attend_kernel, settings), out_shape=out_...  38.1 us
    ppermute x21, starting transfers between devices, swap(): return lax.ppermute(array, axis, [(i, i ^ mask) for i in range(size)])  26.4 us
    pallas_call x2, Pallas kernels, pack(): pl.pallas_call(functools.partial(pack_kernel, wanted, per_peer), out_shap...  10.3 us
    pallas_call x4, Pallas kernels, project(): pl.pallas_call(project_kernel, out_shape=[jax.ShapeDtypeStruct((2, share,...  9.05 us
  transfers between devices with their start and end apart: 21, of which 9 were waited for; matrix products, arithmetic and copies ran while one was open for 5% of the time, Pallas kernels for 41%

commit v1 on v0

--- a/solution.py
+++ b/solution.py
@@ -279,6 +279,30 @@
     )(*state, *parts)
 
 
+def stage_kernel(source, target, sems):
+    rows = source.shape[0] // sems.shape[0]
+    copies = []
+    for n in range(sems.shape[0]):
+        part = pl.ds(n * rows, rows)
+        copies.append(pltpu.make_async_copy(source.at[part], target.at[part], sems.at[n]))
+        copies[-1].start()
+    for copy in copies:
+        copy.wait()
+
+
+def stage(array):
+    return pl.pallas_call(
+        stage_kernel,
+        out_shape=jax.ShapeDtypeStruct(array.shape, array.dtype),
+        in_specs=[pl.BlockSpec(memory_space=pl.ANY)],
+        out_specs=pl.BlockSpec(memory_space=pltpu.VMEM),
+        scratch_shapes=[pltpu.SemaphoreType.DMA((8,))],
+        compiler_params=pltpu.CompilerParams(vmem_limit_bytes=VMEM_SMALL),
+        cost_estimate=COST,
+        name="stage",
+    )(array)
+
+
 def project_kernel(attended, w_mine, w_sooner, w_later, away, keep, scratch):
     core = lax.axis_index("head")
     share = away.shape[1]
@@ -403,6 +427,7 @@
     own = after(own, w_sooner)
     own = attend("attend_own_late", "state", heads, q_mine, valid_mine, some(late), earlier=own)
     w_later = swap(after(w_out[cut:], *own), "req", peers, 1)
+    w_mine = stage(after(w_out, *own))
     own = attend("attend_own_last", "state", heads, q_mine, valid_mine, some(last), earlier=own)
     attended = combine(own, part, heads)
 
@@ -415,13 +440,15 @@
         bit //= 2
 
     single = [m for m in have if m and not m & (m - 1)]
-    results, last = {}, ()
+    w_later = stage(w_later)
+    results, made = {}, []
     for mask in sorted(have, key=lambda m: (m not in single + [0], -m)):
         if mask in single + [0]:
             rows = after(have[mask], *[have[m] for m in single])
         else:
-            rows = after(have[mask], *last, *[results[m] for m in single if m != half])
-        away, keep = last = project(rows, w_out, w_sooner, w_later, cores)
+            rows = after(have[mask], *made)
+        away, keep = project(rows, w_mine, w_sooner, w_later, cores)
+        made += [away, keep]
         away = swap(away, "head", cores, 1)
         summed = (keep + away.astype(jnp.float32)).astype(jnp.bfloat16)
         results[mask] = swap(summed, "req", peers, mask) if mask else summed

time: 143 us -> 139 us (0.972)
  Pallas kernels: 58.8 us -> 54.8 us
  waiting for transfers between devices: 47.3 us -> 50 us
  starting transfers between devices: 26.4 us -> 23.9 us
    pallas_call x4, Pallas kernels: 9.05 us -> 3.16 us  [project(): pl.pallas_call(project_kernel, out_shape=[jax.ShapeDtypeStruct((2, share,...]
    ppermute x21, waiting for transfers between devices: 47.3 us -> 50 us  [swap(): return lax.ppermute(array, axis, [(i, i ^ mask) for i in range(size)])]
    ppermute x21, starting transfers between devices: 26.4 us -> 23.9 us  [swap(): return lax.ppermute(array, axis, [(i, i ^ mask) for i in range(size)])]
    pallas_call x0 -> x2, Pallas kernels: none -> 2.02 us  [stage(): pl.pallas_call(stage_kernel, out_shape=jax.ShapeDtypeStruct(array.shape,...]
  transfers between devices with their start and end apart: 21 -> 21, of which waited for: 9 -> 13; matrix products, arithmetic and copies ran while one was open for 5% -> 5% of each run, Pallas kernels for 41% -> 38%
where the time goes in v1:
time: 139 us
  Pallas kernels  54.8 us (39%)
  waiting for transfers between devices  50 us (36%)
  starting transfers between devices  23.9 us (17%)
  local copies, waits for them, and re-layouts  8.38 us (6%)
    ppermute x21, waiting for transfers between devices, swap(): return lax.ppermute(array, axis, [(i, i ^ mask) for i in range(size)])  50 us
    pallas_call x8, Pallas kernels, attend(): pl.pallas_call(functools.partial(attend_kernel, settings), out_shape=out_...  37.9 us
    ppermute x21, starting transfers between devices, swap(): return lax.ppermute(array, axis, [(i, i ^ mask) for i in range(size)])  23.9 us
    pallas_call x2, Pallas kernels, pack(): pl.pallas_call(functools.partial(pack_kernel, wanted, per_peer), out_shap...  10.3 us
    pallas_call x4, Pallas kernels, project(): pl.pallas_call(project_kernel, out_shape=[jax.ShapeDtypeStruct((2, share,...  3.16 us
    unnamed x28, local copies, waits for them, and re-layouts  3.13 us
  transfers between devices with their start and end apart: 21, of which 13 were waited for; matrix products, arithmetic and copies ran while one was open for 5% of the time, Pallas kernels for 38%

profile of v1, /device:TPU:0, one launch (start us, length us, event | category | flops | bytes accessed | tf_op | source)
XLA Modules:
  0.0 138.7 jit_solution(8664009576406731664)
XLA Ops:
  0.0 4.0 %collective-permute-start = (bf16[2048,128]{1,0:T(8,128)(2,1)}, bf16[2048,128]{1,0:T(8,128)(2,1)S(1)}, u32[]{:S(2)}, u32[]{:S(2)}) collective-permute-start(bf16[2048,128]{1,0:T(8,128)(2,1)} %bitcast.14), channel_id=1, source_target_pairs={{0,8},{2,10},{4,12},{6,14},{8,0},{10,2},{12,4},{14,6},{1,9},{3,11}... | collective-permute-start | bytes 1572872 | tf_op jit(solution)/shard_map/ppermute | solution.py:20
  4.0 4.5 %pack_pieces.2 = (bf16[8,2,128,128]{3,2,1,0:T(8,128)(2,1)}, bf16[8,2,128,128]{3,2,1,0:T(8,128)(2,1)}, bf16[8,2,128,128]{3,2,1,0:T(8,128)(2,1)}) custom-call(s32[16,32]{1,0:T(8,128)} %slot_ref.3, s32[2,8]{1,0:T(2,128)} %bitcast.21, bf16[64,1,2,128,128]{4,3,2,1,0:T(8,128)(2,1)} %kv_ref.2), custom_call_target="tpu_custom_call" | custom-call | flops 1024 | bytes 1024 | tf_op jit(solution)/shard_map/pack_pieces/pallas_call | solution.py:64
  8.6 1.6 %collective-permute-start.1 = (bf16[8,2,128,128]{3,2,1,0:T(8,128)(2,1)}, bf16[8,2,128,128]{3,2,1,0:T(8,128)(2,1)}, u32[]{:S(2)}, u32[]{:S(2)}) collective-permute-start(bf16[8,2,128,128]{3,2,1,0:T(8,128)(2,1)} %get-tuple-element.54), channel_id=1, source_target_pairs={{0,2},{2,0},{4,6},{6,4},{8,10},{10,8},{12,14},{14,12},{1,3},{3,1},... | collective-permute-start | bytes 1572872 | tf_op jit(solution)/shard_map/ppermute | solution.py:20
  10.2 1.6 %collective-permute-start.6 = (bf16[8,2,128,128]{3,2,1,0:T(8,128)(2,1)}, bf16[8,2,128,128]{3,2,1,0:T(8,128)(2,1)S(1)}, u32[]{:S(2)}, u32[]{:S(2)}) collective-permute-start(bf16[8,2,128,128]{3,2,1,0:T(8,128)(2,1)} %get-tuple-element.55), channel_id=1, source_target_pairs={{0,4},{2,6},{4,0},{6,2},{8,12},{10,14},{12,8},{14,10},{1,5},{3,7},... | collective-permute-start | bytes 1572872 | tf_op jit(solution)/shard_map/ppermute | solution.py:20
  11.7 0.4 collective-permute-start.5
  12.2 0.2 dynamic-slice_reduce_fusion
  12.4 0.6 gather_fusion
  13.0 0.6 gather_fusion.3
  13.6 0.6 gather_fusion.2
  14.2 0.6 gather_fusion.5
  14.8 0.5 convert_reduce_fusion
  15.3 0.6 gather_fusion.1
  16.1 5.8 %pack_pieces.3 = (bf16[8,2,128,128]{3,2,1,0:T(8,128)(2,1)}, bf16[8,2,128,128]{3,2,1,0:T(8,128)(2,1)}, bf16[8,2,128,128]{3,2,1,0:T(8,128)(2,1)}, bf16[8,2,128,128]{3,2,1,0:T(8,128)(2,1)}, bf16[8,2,128,128]{3,2,1,0:T(8,128)(2,1)}) custom-call(s32[16,32]{1,0:T(8,128)} %slot_ref.3, s32[2,8]{1,0:T(2,128)} %bitcast.22, bf16[64,1,2,128,128]{4,3,2,1,0:T(8,128)(2,1)} %kv_ref.2), custom_call_target="tpu_custom_call" | custom-call | flops 1024 | bytes 1024 | tf_op jit(solution)/shard_map/pack_pieces/pallas_call | solution.py:64
  21.8 0.2 select_reduce_fusion.1
  22.1 0.1 reshape.175.refs_1_
  22.2 1.0 copy-done.5
  23.2 5.3 %attend_own_local.1 = (f32[2048,128]{1,0:T(8,128)S(1)}, f32[4,4,128]{2,1,0:T(4,128)S(1)}) custom-call(bf16[2048,128]{1,0:T(8,128)(2,1)S(1)} %bitcast.15, s32[4,8]{1,0:T(4,128)S(1)} %reshape.175.refs_1_, bf16[128,128]{1,0:T(8,128)(2,1)S(1)} %bitcast.19, bf16[128,128]{1,0:T(8,128)(2,1)S(1)} %bitcast.20, bf16[8,2,128,128]{3,2,1,0:T(8,128)(2,1)S(1)} %copy-done.5), custom_call_target="tpu_custom_call" | custom-call | flops 1024 | bytes 1024 | tf_op jit(solution)/shard_map/attend_own_local/pallas_call | solution.py:230
  28.5 0.6 gather_fusion.4
  29.1 0.2 select_reduce_fusion
  29.3 0.1 reshape.176.refs_1_
  29.4 1.0 copy-done.8
  30.5 4.1 %attend_partner_local.1 = (f32[2048,128]{1,0:T(8,128)S(1)}, f32[4,4,128]{2,1,0:T(4,128)S(1)}) custom-call(bf16[2048,128]{1,0:T(8,128)(2,1)S(1)} %collective-permute-done.refs_0_, s32[4,8]{1,0:T(4,128)S(1)} %reshape.176.refs_1_, bf16[8,2,128,128]{3,2,1,0:T(8,128)(2,1)S(1)} %copy-done.8), custom_call_target="tpu_custom_call" | custom-call | flops 2147483648 | bytes 1024 | tf_op jit(solution)/shard_map/attend_partner_local/pallas_call | solution.py:230
  34.6 5.1 %attend_partner_early.1 = (f32[2048,128]{1,0:T(8,128)S(1)}, f32[4,4,128]{2,1,0:T(4,128)S(1)}) custom-call(bf16[2048,128]{1,0:T(8,128)(2,1)S(1)} %collective-permute-done.refs_0_, s32[4,8]{1,0:T(4,128)S(1)} %reshape.176.refs_1_, bf16[8,2,128,128]{3,2,1,0:T(8,128)(2,1)} %collective-permute-done.1.refs_2_, f32[2048,128]{1,0:T(8,128)S(1)} %get-tuple-element.64.refs_3_, ...), custom_call_target="tpu_custom_call" | custom-call | flops 1024 | bytes 1024 | tf_op jit(solution)/shard_map/attend_partner_early/pallas_call | solution.py:230
  39.8 1.6 %collective-permute-start.4 = (bf16[8,2,128,128]{3,2,1,0:T(8,128)(2,1)S(1)}, bf16[8,2,128,128]{3,2,1,0:T(8,128)(2,1)S(1)}, u32[]{:S(2)}, u32[]{:S(2)}) collective-permute-start(bf16[8,2,128,128]{3,2,1,0:T(8,128)(2,1)S(1)} %copy-done.13), channel_id=1, source_target_pairs={{0,2},{2,0},{4,6},{6,4},{8,10},{10,8},{12,14},{14,12},{1,3},{3,1},... | collective-permute-start | bytes 1572872 | tf_op jit(solution)/shard_map/ppermute | solution.py:20
  41.4 1.6 %collective-permute-start.3 = (bf16[8,2,128,128]{3,2,1,0:T(8,128)(2,1)S(1)}, bf16[8,2,128,128]{3,2,1,0:T(8,128)(2,1)S(1)}, u32[]{:S(2)}, u32[]{:S(2)}) collective-permute-start(bf16[8,2,128,128]{3,2,1,0:T(8,128)(2,1)S(1)} %copy-done.12), channel_id=1, source_target_pairs={{0,4},{2,6},{4,0},{6,2},{8,12},{10,14},{12,8},{14,10},{1,5},{3,7},... | collective-permute-start | bytes 1572872 | tf_op jit(solution)/shard_map/ppermute | solution.py:20
  42.9 0.4 collective-permute-start.2
  43.4 4.6 %attend_partner_late.1 = (f32[2048,128]{1,0:T(8,128)S(1)}, f32[4,4,128]{2,1,0:T(4,128)S(1)}) custom-call(bf16[2048,128]{1,0:T(8,128)(2,1)S(1)} %collective-permute-done.refs_0_, s32[4,8]{1,0:T(4,128)S(1)} %reshape.176.refs_1_, bf16[8,2,128,128]{3,2,1,0:T(8,128)(2,1)S(1)} %collective-permute-done.6.refs_2_, f32[2048,128]{1,0:T(8,128)S(1)} %get-tuple-element.66.refs_3_, ...), custom_call_target="tpu_custom_call" | custom-call | flops 1024 | bytes 1024 | tf_op jit(solution)/shard_map/attend_partner_late/pallas_call | solution.py:230
  47.9 5.1 %attend_partner_last.1 = (bf16[1072,128]{1,0:T(8,128)(2,1)S(1)}, bf16[1024,128]{1,0:T(8,128)(2,1)S(1)}) custom-call(bf16[2048,128]{1,0:T(8,128)(2,1)S(1)} %collective-permute-done.refs_0_, s32[4,8]{1,0:T(4,128)S(1)} %reshape.176.refs_1_, bf16[8,2,128,128]{3,2,1,0:T(8,128)(2,1)S(1)} %collective-permute-done.5.refs_2_, ...), custom_call_target="tpu_custom_call" | custom-call | flops 1024 | bytes 1024 | tf_op jit(solution)/shard_map/attend_partner_last/pallas_call | solution.py:230
  53.0 1.6 %collective-permute-start.7 = (bf16[384,512]{1,0:T(8,128)(2,1)S(1)}, bf16[384,512]{1,0:T(8,128)(2,1)S(1)}, u32[]{:S(2)}, u32[]{:S(2)}) collective-permute-start(bf16[384,512]{1,0:T(8,128)(2,1)S(1)} %slice.6), channel_id=1, source_target_pairs={{0,2},{2,0},{4,6},{6,4},{8,10},{10,8},{12,14},{14,12},{1,3},{3,1},... | collective-permute-start | bytes 1179656 | tf_op jit(solution)/shard_map/ppermute | solution.py:20
  54.6 0.3 collective-permute-start.8
  54.9 2.0 %collective-permute-done.4.refs_2_ = bf16[8,2,128,128]{3,2,1,0:T(8,128)(2,1)S(1)} collective-permute-done((bf16[8,2,128,128]{3,2,1,0:T(8,128)(2,1)S(1)}, bf16[8,2,128,128]{3,2,1,0:T(8,128)(2,1)S(1)}, u32[]{:S(2)}, u32[]{:S(2)}) %collective-permute-start.4) | collective-permute-done | bytes 524320 | tf_op jit(solution)/shard_map/ppermute | solution.py:20
  56.9 0.6 collective-permute-start.9
  57.5 1.3 slice.7
  58.9 4.6 %attend_own_early.1 = (f32[2048,128]{1,0:T(8,128)S(1)}, f32[4,4,128]{2,1,0:T(4,128)S(1)}) custom-call(bf16[2048,128]{1,0:T(8,128)(2,1)S(1)} %bitcast.16, s32[4,8]{1,0:T(4,128)S(1)} %reshape.175.refs_1_, bf16[8,2,128,128]{3,2,1,0:T(8,128)(2,1)S(1)} %collective-permute-done.4.refs_2_, f32[2048,128]{1,0:T(8,128)S(1)} %get-tuple-element.77.refs_3_, ...), custom_call_target="tpu_custom_call" | custom-call | flops 1024 | bytes 1024 | tf_op jit(solution)/shard_map/attend_own_early/pallas_call | solution.py:230
  63.4 2.0 %collective-permute-done.7.w_sooner = bf16[384,512]{1,0:T(8,128)(2,1)S(1)} collective-permute-done((bf16[384,512]{1,0:T(8,128)(2,1)S(1)}, bf16[384,512]{1,0:T(8,128)(2,1)S(1)}, u32[]{:S(2)}, u32[]{:S(2)}) %collective-permute-start.7) | collective-permute-done | bytes 393248 | tf_op jit(solution)/shard_map/ppermute | solution.py:20
  65.5 2.4 %collective-permute-done.3.refs_2_ = bf16[8,2,128,128]{3,2,1,0:T(8,128)(2,1)S(1)} collective-permute-done((bf16[8,2,128,128]{3,2,1,0:T(8,128)(2,1)S(1)}, bf16[8,2,128,128]{3,2,1,0:T(8,128)(2,1)S(1)}, u32[]{:S(2)}, u32[]{:S(2)}) %collective-permute-start.3) | collective-permute-done | bytes 524320 | tf_op jit(solution)/shard_map/ppermute | solution.py:20
  67.8 4.6 %attend_own_late.1 = (f32[2048,128]{1,0:T(8,128)S(1)}, f32[4,4,128]{2,1,0:T(4,128)S(1)}) custom-call(bf16[2048,128]{1,0:T(8,128)(2,1)S(1)} %bitcast.17, s32[4,8]{1,0:T(4,128)S(1)} %reshape.175.refs_1_, bf16[8,2,128,128]{3,2,1,0:T(8,128)(2,1)S(1)} %collective-permute-done.3.refs_2_, f32[2048,128]{1,0:T(8,128)S(1)} %get-tuple-element.82.refs_3_, ...), custom_call_target="tpu_custom_call" | custom-call | flops 1024 | bytes 1024 | tf_op jit(solution)/shard_map/attend_own_late/pallas_call | solution.py:230
  72.4 0.6 collective-permute-start.12
  73.0 4.4 %collective-permute-done.2.refs_2_ = bf16[8,2,128,128]{3,2,1,0:T(8,128)(2,1)S(1)} collective-permute-done((bf16[8,2,128,128]{3,2,1,0:T(8,128)(2,1)S(1)}, bf16[8,2,128,128]{3,2,1,0:T(8,128)(2,1)S(1)}, u32[]{:S(2)}, u32[]{:S(2)}) %collective-permute-start.2) | collective-permute-done | bytes 524320 | tf_op jit(solution)/shard_map/ppermute | solution.py:20
  77.4 4.6 %attend_own_last.1 = (f32[2048,128]{1,0:T(8,128)S(1)}, f32[4,4,128]{2,1,0:T(4,128)S(1)}) custom-call(bf16[2048,128]{1,0:T(8,128)(2,1)S(1)} %bitcast.18, s32[4,8]{1,0:T(4,128)S(1)} %reshape.175.refs_1_, bf16[8,2,128,128]{3,2,1,0:T(8,128)(2,1)S(1)} %collective-permute-done.2.refs_2_, f32[2048,128]{1,0:T(8,128)S(1)} %get-tuple-element.84.refs_3_, ...), custom_call_target="tpu_custom_call" | custom-call | flops 1024 | bytes 1024 | tf_op jit(solution)/shard_map/attend_own_last/pallas_call | solution.py:230
  82.0 0.6 combine.1.attended
  82.6 3.2 %collective-permute-start.10 = (bf16[128,2048]{1,0:T(8,128)(2,1)S(1)}, bf16[128,2048]{1,0:T(8,128)(2,1)S(1)}, u32[]{:S(2)}, u32[]{:S(2)}) collective-permute-start(bf16[128,2048]{1,0:T(8,128)(2,1)S(1)} %combine.1.attended), channel_id=1, source_target_pairs={{0,8},{2,10},{4,12},{6,14},{8,0},{10,2},{12,4},{14,6},{1,9},{3,11}... | collective-permute-start | bytes 1572872 | tf_op jit(solution)/shard_map/ppermute | solution.py:20
  85.7 22.5 %collective-permute-done.10.attended = bf16[128,2048]{1,0:T(8,128)(2,1)S(1)} collective-permute-done((bf16[128,2048]{1,0:T(8,128)(2,1)S(1)}, bf16[128,2048]{1,0:T(8,128)(2,1)S(1)}, u32[]{:S(2)}, u32[]{:S(2)}) %collective-permute-start.10) | collective-permute-done | bytes 524320 | tf_op jit(solution)/shard_map/ppermute | solution.py:20
  108.3 0.5 collective-permute-done.11.attended
  108.8 1.2 collective-permute-start.18
  110.0 0.4 stage.2.w_mine
  110.4 3.5 %collective-permute-done.12.source = bf16[1664,512]{1,0:T(8,128)(2,1)} collective-permute-done((bf16[1664,512]{1,0:T(8,128)(2,1)}, bf16[1664,512]{1,0:T(8,128)(2,1)}, u32[]{:S(2)}, u32[]{:S(2)}) %collective-permute-start.12) | collective-permute-done | bytes 1703968 | tf_op jit(solution)/shard_map/ppermute | solution.py:20
  113.9 1.6 %stage.3.w_later = bf16[1664,512]{1,0:T(8,128)(2,1)S(1)} custom-call(bf16[1664,512]{1,0:T(8,128)(2,1)} %collective-permute-done.12.source), custom_call_target="tpu_custom_call" | custom-call | flops 1024 | bytes 1024 | tf_op jit(solution)/shard_map/stage/pallas_call | solution.py:294
  115.5 0.8 project.6
  116.3 1.0 copy-done.4
  117.3 0.8 project.5
  118.1 0.8 project.4
  118.9 2.3 %collective-permute-done.18.attended = bf16[128,2048]{1,0:T(8,128)(2,1)S(1)} collective-permute-done((bf16[128,2048]{1,0:T(8,128)(2,1)S(1)}, bf16[128,2048]{1,0:T(8,128)(2,1)S(1)}, u32[]{:S(2)}, u32[]{:S(2)}) %collective-permute-start.18) | collective-permute-done | bytes 524320 | tf_op jit(solution)/shard_map/ppermute | solution.py:20
  121.2 0.8 project.7
  122.1 0.5 collective-permute-start.17
  122.7 0.4 collective-permute-start.13
  123.1 0.3 collective-permute-done.19
  123.6 0.4 collective-permute-done.15
  124.0 1.9 %collective-permute-start.16 = (bf16[2,64,512]{2,1,0:T(8,128)(2,1)S(1)}, bf16[2,64,512]{2,1,0:T(8,128)(2,1)S(1)}, u32[]{:S(2)}, u32[]{:S(2)}) collective-permute-start(bf16[2,64,512]{2,1,0:T(8,128)(2,1)S(1)} %add_convert_fusion.2), channel_id=1, source_target_pairs={{0,4},{2,6},{4,0},{6,2},{8,12},{10,14},{12,8},{14,10},{1,5},{3,7},... | collective-permute-start | bytes 393224 | tf_op jit(solution)/shard_map/ppermute | solution.py:20
  126.0 2.2 %collective-permute-start.14 = (bf16[2,64,512]{2,1,0:T(8,128)(2,1)S(1)}, bf16[2,64,512]{2,1,0:T(8,128)(2,1)S(1)}, u32[]{:S(2)}, u32[]{:S(2)}) collective-permute-start(bf16[2,64,512]{2,1,0:T(8,128)(2,1)S(1)} %add_convert_fusion.3), channel_id=1, source_target_pairs={{0,8},{2,10},{4,12},{6,14},{8,0},{10,2},{12,4},{14,6},{1,9},{3,11}... | collective-permute-start | bytes 393224 | tf_op jit(solution)/shard_map/ppermute | solution.py:20
  128.2 3.6 %collective-permute-done.20.refs_3_ = bf16[2,64,512]{2,1,0:T(8,128)(2,1)S(1)} collective-permute-done((bf16[2,64,512]{2,1,0:T(8,128)(2,1)S(1)}, bf16[2,64,512]{2,1,0:T(8,128)(2,1)S(1)}, u32[]{:S(2)}, u32[]{:S(2)}) %collective-permute-start.20) | collective-permute-done | bytes 131104 | tf_op jit(solution)/shard_map/ppermute | solution.py:20
  131.7 1.7 %collective-permute-done.16.refs_1_ = bf16[2,64,512]{2,1,0:T(8,128)(2,1)S(1)} collective-permute-done((bf16[2,64,512]{2,1,0:T(8,128)(2,1)S(1)}, bf16[2,64,512]{2,1,0:T(8,128)(2,1)S(1)}, u32[]{:S(2)}, u32[]{:S(2)}) %collective-permute-start.16) | collective-permute-done | bytes 131104 | tf_op jit(solution)/shard_map/ppermute | solution.py:20
  133.5 4.4 %collective-permute-done.14.refs_0_ = bf16[2,64,512]{2,1,0:T(8,128)(2,1)S(1)} collective-permute-done((bf16[2,64,512]{2,1,0:T(8,128)(2,1)S(1)}, bf16[2,64,512]{2,1,0:T(8,128)(2,1)S(1)}, u32[]{:S(2)}, u32[]{:S(2)}) %collective-permute-start.14) | collective-permute-done | bytes 131104 | tf_op jit(solution)/shard_map/ppermute | solution.py:20
  137.8 0.8 place_columns.1
  (53 shorter events, 0.6 us)
Async XLA Ops:
  0.0 13.6 %copy-start = (s32[16]{0:T(128)S(1)}, s32[16]{0:T(128)}, u32[]{:S(2)}) copy-start(s32[16]{0:T(128)} %param.12) | copy-start | bytes 196
  0.0 29.4 %collective-permute-start = (bf16[2048,128]{1,0:T(8,128)(2,1)}, bf16[2048,128]{1,0:T(8,128)(2,1)S(1)}, u32[]{:S(2)}, u32[]{:S(2)}) collective-permute-start(bf16[2048,128]{1,0:T(8,128)(2,1)} %bitcast.14), channel_id=1, source_target_pairs={{0,8},{2,10},{4,12},{6,14},{8,0},{10,2},{12,4},{14,6},{1,9},{3,11}... | collective-permute-start | bytes 1572872 | tf_op jit(solution)/shard_map/ppermute | solution.py:20
  4.0 8.1 %copy-start.9 = (s32[16,32]{1,0:T(8,128)S(1)}, s32[16,32]{1,0:T(8,128)}, u32[]{:S(2)}) copy-start(s32[16,32]{1,0:T(8,128)} %slot_ref.3) | copy-start | bytes 6148
  4.0 8.1 %copy-start.10 = (s32[8,1,2]{0,2,1:T(2,128)S(1)}, s32[8,1,2]{0,2,1:T(2,128)}, u32[]{:S(2)}) copy-start(s32[8,1,2]{0,2,1:T(2,128)} %param.14) | copy-start | bytes 196
  8.6 26.0 %collective-permute-start.1 = (bf16[8,2,128,128]{3,2,1,0:T(8,128)(2,1)}, bf16[8,2,128,128]{3,2,1,0:T(8,128)(2,1)}, u32[]{:S(2)}, u32[]{:S(2)}) collective-permute-start(bf16[8,2,128,128]{3,2,1,0:T(8,128)(2,1)} %get-tuple-element.54), channel_id=1, source_target_pairs={{0,2},{2,0},{4,6},{6,4},{8,10},{10,8},{12,14},{14,12},{1,3},{3,1},... | collective-permute-start | bytes 1572872 | tf_op jit(solution)/shard_map/ppermute | solution.py:20
  10.2 33.2 %collective-permute-start.6 = (bf16[8,2,128,128]{3,2,1,0:T(8,128)(2,1)}, bf16[8,2,128,128]{3,2,1,0:T(8,128)(2,1)S(1)}, u32[]{:S(2)}, u32[]{:S(2)}) collective-permute-start(bf16[8,2,128,128]{3,2,1,0:T(8,128)(2,1)} %get-tuple-element.55), channel_id=1, source_target_pairs={{0,4},{2,6},{4,0},{6,2},{8,12},{10,14},{12,8},{14,10},{1,5},{3,7},... | collective-permute-start | bytes 1572872 | tf_op jit(solution)/shard_map/ppermute | solution.py:20
  11.7 36.2 %collective-permute-start.5 = (bf16[8,2,128,128]{3,2,1,0:T(8,128)(2,1)}, bf16[8,2,128,128]{3,2,1,0:T(8,128)(2,1)S(1)}, u32[]{:S(2)}, u32[]{:S(2)}) collective-permute-start(bf16[8,2,128,128]{3,2,1,0:T(8,128)(2,1)} %get-tuple-element.56), channel_id=1, source_target_pairs={{0,6},{2,4},{4,2},{6,0},{8,14},{10,12},{12,10},{14,8},{1,7},{3,5},... | collective-permute-start | bytes 1572872 | tf_op jit(solution)/shard_map/ppermute | solution.py:20
  16.0 6.1 %copy-start.1 = (bf16[128,16,128]{2,1,0:T(8,128)(2,1)S(1)}, bf16[128,16,128]{2,1,0:T(8,128)(2,1)}, u32[]{:S(2)}) copy-start(bf16[128,16,128]{2,1,0:T(8,128)(2,1)} %param.8) | copy-start | bytes 1572868
  16.0 6.1 %copy-start.6 = (bf16[128,1,128]{2,0,1:T(8,128)(2,1)S(1)}, bf16[128,1,128]{2,0,1:T(8,128)(2,1)}, u32[]{:S(2)}) copy-start(bf16[128,1,128]{2,0,1:T(8,128)(2,1)} %param.9) | copy-start | bytes 98308
  16.1 6.1 %copy-start.7 = (bf16[128,1,128]{2,0,1:T(8,128)(2,1)S(1)}, bf16[128,1,128]{2,0,1:T(8,128)(2,1)}, u32[]{:S(2)}) copy-start(bf16[128,1,128]{2,0,1:T(8,128)(2,1)} %param.10) | copy-start | bytes 98308
  22.2 1.0 copy-start.5
  29.4 1.0 copy-start.8
  30.5 9.3 %copy-start.13 = (bf16[8,2,128,128]{3,2,1,0:T(8,128)(2,1)S(1)}, bf16[8,2,128,128]{3,2,1,0:T(8,128)(2,1)}, u32[]{:S(2)}) copy-start(bf16[8,2,128,128]{3,2,1,0:T(8,128)(2,1)} %get-tuple-element.72) | copy-start | bytes 1572868
  30.5 10.9 %copy-start.12 = (bf16[8,2,128,128]{3,2,1,0:T(8,128)(2,1)S(1)}, bf16[8,2,128,128]{3,2,1,0:T(8,128)(2,1)}, u32[]{:S(2)}) copy-start(bf16[8,2,128,128]{3,2,1,0:T(8,128)(2,1)} %get-tuple-element.70) | copy-start | bytes 1572868
  30.5 12.5 %copy-start.11 = (bf16[8,2,128,128]{3,2,1,0:T(8,128)(2,1)S(1)}, bf16[8,2,128,128]{3,2,1,0:T(8,128)(2,1)}, u32[]{:S(2)}) copy-start(bf16[8,2,128,128]{3,2,1,0:T(8,128)(2,1)} %get-tuple-element.68) | copy-start | bytes 1572868
  34.6 8.7 %copy-start.2 = (bf16[2048,512]{1,0:T(8,128)(2,1)S(1)}, bf16[2048,512]{1,0:T(8,128)(2,1)}, u32[]{:S(2)}) copy-start(bf16[2048,512]{1,0:T(8,128)(2,1)} %source) | copy-start | bytes 6291460
  39.8 17.2 %collective-permute-start.4 = (bf16[8,2,128,128]{3,2,1,0:T(8,128)(2,1)S(1)}, bf16[8,2,128,128]{3,2,1,0:T(8,128)(2,1)S(1)}, u32[]{:S(2)}, u32[]{:S(2)}) collective-permute-start(bf16[8,2,128,128]{3,2,1,0:T(8,128)(2,1)S(1)} %copy-done.13), channel_id=1, source_target_pairs={{0,2},{2,0},{4,6},{6,4},{8,10},{10,8},{12,14},{14,12},{1,3},{3,1},... | collective-permute-start | bytes 1572872 | tf_op jit(solution)/shard_map/ppermute | solution.py:20
  41.4 26.4 %collective-permute-start.3 = (bf16[8,2,128,128]{3,2,1,0:T(8,128)(2,1)S(1)}, bf16[8,2,128,128]{3,2,1,0:T(8,128)(2,1)S(1)}, u32[]{:S(2)}, u32[]{:S(2)}) collective-permute-start(bf16[8,2,128,128]{3,2,1,0:T(8,128)(2,1)S(1)} %copy-done.12), channel_id=1, source_target_pairs={{0,4},{2,6},{4,0},{6,2},{8,12},{10,14},{12,8},{14,10},{1,5},{3,7},... | collective-permute-start | bytes 1572872 | tf_op jit(solution)/shard_map/ppermute | solution.py:20
  42.9 34.5 %collective-permute-start.2 = (bf16[8,2,128,128]{3,2,1,0:T(8,128)(2,1)S(1)}, bf16[8,2,128,128]{3,2,1,0:T(8,128)(2,1)S(1)}, u32[]{:S(2)}, u32[]{:S(2)}) collective-permute-start(bf16[8,2,128,128]{3,2,1,0:T(8,128)(2,1)S(1)} %copy-done.11), channel_id=1, source_target_pairs={{0,6},{2,4},{4,2},{6,0},{8,14},{10,12},{12,10},{14,8},{1,7},{3,5},... | collective-permute-start | bytes 1572872 | tf_op jit(solution)/shard_map/ppermute | solution.py:20
  53.0 12.4 %collective-permute-start.7 = (bf16[384,512]{1,0:T(8,128)(2,1)S(1)}, bf16[384,512]{1,0:T(8,128)(2,1)S(1)}, u32[]{:S(2)}, u32[]{:S(2)}) collective-permute-start(bf16[384,512]{1,0:T(8,128)(2,1)S(1)} %slice.6), channel_id=1, source_target_pairs={{0,2},{2,0},{4,6},{6,4},{8,10},{10,8},{12,14},{14,12},{1,3},{3,1},... | collective-permute-start | bytes 1179656 | tf_op jit(solution)/shard_map/ppermute | solution.py:20
  54.6 27.4 %collective-permute-start.8 = (bf16[1072,128]{1,0:T(8,128)(2,1)S(1)}, bf16[1072,128]{1,0:T(8,128)(2,1)S(1)}, u32[]{:S(2)}, u32[]{:S(2)}) collective-permute-start(bf16[1072,128]{1,0:T(8,128)(2,1)S(1)} %get-tuple-element.75), channel_id=1, source_target_pairs={{0,8},{2,10},{4,12},{6,14},{8,0},{10,2},{12,4},{14,6},{1,9},{3,11}... | collective-permute-start | bytes 823304 | tf_op jit(solution)/shard_map/ppermute | solution.py:20
  56.9 25.0 %collective-permute-start.9 = (bf16[1024,128]{1,0:T(8,128)(2,1)S(1)}, bf16[1024,128]{1,0:T(8,128)(2,1)S(1)}, u32[]{:S(2)}, u32[]{:S(2)}) collective-permute-start(bf16[1024,128]{1,0:T(8,128)(2,1)S(1)} %get-tuple-element.76), channel_id=1, source_target_pairs={{0,8},{2,10},{4,12},{6,14},{8,0},{10,2},{12,4},{14,6},{1,9},{3,11}... | collective-permute-start | bytes 786440 | tf_op jit(solution)/shard_map/ppermute | solution.py:20
  65.5 50.0 %copy-start.3 = (bf16[384,512]{1,0:T(8,128)(2,1)}, bf16[384,512]{1,0:T(8,128)(2,1)S(1)}, u32[]{:S(2)}) copy-start(bf16[384,512]{1,0:T(8,128)(2,1)S(1)} %collective-permute-done.7.w_sooner) | copy-start | bytes 1179652
  72.4 41.5 %collective-permute-start.12 = (bf16[1664,512]{1,0:T(8,128)(2,1)}, bf16[1664,512]{1,0:T(8,128)(2,1)}, u32[]{:S(2)}, u32[]{:S(2)}) collective-permute-start(bf16[1664,512]{1,0:T(8,128)(2,1)} %slice.7), channel_id=1, source_target_pairs={{0,2},{2,0},{4,6},{6,4},{8,10},{10,8},{12,14},{14,12},{1,3},{3,1},... | collective-permute-start | bytes 5111816 | tf_op jit(solution)/shard_map/ppermute | solution.py:20
  82.6 25.7 %collective-permute-start.10 = (bf16[128,2048]{1,0:T(8,128)(2,1)S(1)}, bf16[128,2048]{1,0:T(8,128)(2,1)S(1)}, u32[]{:S(2)}, u32[]{:S(2)}) collective-permute-start(bf16[128,2048]{1,0:T(8,128)(2,1)S(1)} %combine.1.attended), channel_id=1, source_target_pairs={{0,8},{2,10},{4,12},{6,14},{8,0},{10,2},{12,4},{14,6},{1,9},{3,11}... | collective-permute-start | bytes 1572872 | tf_op jit(solution)/shard_map/ppermute | solution.py:20
  85.7 23.0 %collective-permute-start.11 = (bf16[128,2048]{1,0:T(8,128)(2,1)S(1)}, bf16[128,2048]{1,0:T(8,128)(2,1)S(1)}, u32[]{:S(2)}, u32[]{:S(2)}) collective-permute-start(bf16[128,2048]{1,0:T(8,128)(2,1)S(1)} %combine.1.attended), channel_id=1, source_target_pairs={{0,4},{2,6},{4,0},{6,2},{8,12},{10,14},{12,8},{14,10},{1,5},{3,7},... | collective-permute-start | bytes 1572872 | tf_op jit(solution)/shard_map/ppermute | solution.py:20
  108.8 12.5 %collective-permute-start.18 = (bf16[128,2048]{1,0:T(8,128)(2,1)S(1)}, bf16[128,2048]{1,0:T(8,128)(2,1)S(1)}, u32[]{:S(2)}, u32[]{:S(2)}) collective-permute-start(bf16[128,2048]{1,0:T(8,128)(2,1)S(1)} %collective-permute-done.10.attended), channel_id=1, source_target_pairs={{0,4},{2,6},{4,0},{6,2},{8,12},{10,14},{12,8},{14,10},{1,5},{3,7},... | collective-permute-start | bytes 1572872 | tf_op jit(solution)/shard_map/ppermute | solution.py:20
  116.3 1.0 copy-start.4
  122.0 1.4 %collective-permute-start.19 = (bf16[2,64,512]{2,1,0:T(8,128)(2,1)S(1)}, bf16[2,64,512]{2,1,0:T(8,128)(2,1)S(1)}, u32[]{:S(2)}, u32[]{:S(2)}) collective-permute-start(bf16[2,64,512]{2,1,0:T(8,128)(2,1)S(1)} %get-tuple-element.102), channel_id=1, source_target_pairs={{0,1},{1,0},{2,3},{3,2},{4,5},{5,4},{6,7},{7,6},{8,9},{9,8},{10,11... | collective-permute-start | bytes 393224 | tf_op jit(solution)/shard_map/ppermute | solution.py:20
  122.1 6.0 %collective-permute-start.17 = (bf16[2,64,512]{2,1,0:T(8,128)(2,1)S(1)}, bf16[2,64,512]{2,1,0:T(8,128)(2,1)S(1)}, u32[]{:S(2)}, u32[]{:S(2)}) collective-permute-start(bf16[2,64,512]{2,1,0:T(8,128)(2,1)S(1)} %get-tuple-element.98), channel_id=1, source_target_pairs={{0,1},{1,0},{2,3},{3,2},{4,5},{5,4},{6,7},{7,6},{8,9},{9,8},{10,11... | collective-permute-start | bytes 393224 | tf_op jit(solution)/shard_map/ppermute | solution.py:20
  122.6 1.3 collective-permute-start.15
  122.7 3.2 %collective-permute-start.13 = (bf16[2,64,512]{2,1,0:T(8,128)(2,1)S(1)}, bf16[2,64,512]{2,1,0:T(8,128)(2,1)S(1)}, u32[]{:S(2)}, u32[]{:S(2)}) collective-permute-start(bf16[2,64,512]{2,1,0:T(8,128)(2,1)S(1)} %get-tuple-element.92), channel_id=1, source_target_pairs={{0,1},{1,0},{2,3},{3,2},{4,5},{5,4},{6,7},{7,6},{8,9},{9,8},{10,11... | collective-permute-start | bytes 393224 | tf_op jit(solution)/shard_map/ppermute | solution.py:20
  123.5 8.2 %collective-permute-start.20 = (bf16[2,64,512]{2,1,0:T(8,128)(2,1)S(1)}, bf16[2,64,512]{2,1,0:T(8,128)(2,1)S(1)}, u32[]{:S(2)}, u32[]{:S(2)}) collective-permute-start(bf16[2,64,512]{2,1,0:T(8,128)(2,1)S(1)} %add_convert_fusion), channel_id=1, source_target_pairs={{0,12},{2,14},{4,8},{6,10},{8,4},{10,6},{12,0},{14,2},{1,13},{3,15... | collective-permute-start | bytes 393224 | tf_op jit(solution)/shard_map/ppermute | solution.py:20
  124.0 9.5 %collective-permute-start.16 = (bf16[2,64,512]{2,1,0:T(8,128)(2,1)S(1)}, bf16[2,64,512]{2,1,0:T(8,128)(2,1)S(1)}, u32[]{:S(2)}, u32[]{:S(2)}) collective-permute-start(bf16[2,64,512]{2,1,0:T(8,128)(2,1)S(1)} %add_convert_fusion.2), channel_id=1, source_target_pairs={{0,4},{2,6},{4,0},{6,2},{8,12},{10,14},{12,8},{14,10},{1,5},{3,7},... | collective-permute-start | bytes 393224 | tf_op jit(solution)/shard_map/ppermute | solution.py:20
  126.0 11.9 %collective-permute-start.14 = (bf16[2,64,512]{2,1,0:T(8,128)(2,1)S(1)}, bf16[2,64,512]{2,1,0:T(8,128)(2,1)S(1)}, u32[]{:S(2)}, u32[]{:S(2)}) collective-permute-start(bf16[2,64,512]{2,1,0:T(8,128)(2,1)S(1)} %add_convert_fusion.3), channel_id=1, source_target_pairs={{0,8},{2,10},{4,12},{6,14},{8,0},{10,2},{12,4},{14,6},{1,9},{3,11}... | collective-permute-start | bytes 393224 | tf_op jit(solution)/shard_map/ppermute | solution.py:20

commit v2 on v1

--- a/solution.py
+++ b/solution.py
@@ -35,23 +35,25 @@
     held = kv_ref.shape[0]
     picks = ids.shape[0]
     low = me * held
+    chosen = [ids[s, me ^ mask] for mask in wanted for s in range(picks)]
+
+    def scan(p, counts):
+        later = []
+        for row, (c, count) in enumerate(zip(chosen, counts)):
+            slot = slots[c, p] - low
+            table[row, count] = slot
+            later.append(count + ((slot >= 0) & (slot < held)).astype(jnp.int32))
+        return tuple(later)
+
+    lax.fori_loop(0, pieces, scan, (jnp.int32(0),) * len(chosen), unroll=4)
     copies = []
-    for out, mask in zip(outs, wanted):
-        for s in range(picks):
-            row = (len(copies) // per_peer) % table.shape[0]
-            c = ids[s, me ^ mask]
-
-            def scan(p, count, c=c, row=row):
-                slot = slots[c, p] - low
-                table[row, count] = slot
-                return count + ((slot >= 0) & (slot < held)).astype(jnp.int32)
-
-            lax.fori_loop(0, pieces, scan, jnp.int32(0), unroll=8)
-            for k in range(per_peer):
-                copies.append(
-                    pltpu.make_async_copy(kv_ref.at[table[row, k], 0], out.at[s * per_peer + k], sems.at[len(copies)])
-                )
-                copies[-1].start()
+    for row in range(len(chosen)):
+        out, s = outs[row // picks], row % picks
+        for k in range(per_peer):
+            copies.append(
+                pltpu.make_async_copy(kv_ref.at[table[row, k], 0], out.at[s * per_peer + k], sems.at[len(copies)])
+            )
+            copies[-1].start()
     for copy in copies:
         copy.wait()
 
@@ -407,7 +409,8 @@
         return {m: got[m] for m in chosen}
 
     own = attend(
-        "attend_own_local", "state", heads, q_mine, valid_mine, {0: own_pieces}, (new_keys[:, 0], new_values[:, 0])
+        "attend_own_local", "state", heads, after(q_mine, valid_theirs, got[0]), valid_mine, {0: own_pieces},
+        (new_keys[:, 0], new_values[:, 0]),
     )
     q_theirs = after(q_theirs, *own)
     state = attend("attend_partner_local", "state", heads, q_theirs, valid_theirs, some([0]), cost=SHORT)

time: 139 us -> 139 us (level)
  waiting for transfers between devices: 50 us -> 45.2 us
  starting transfers between devices: 23.9 us -> 28.1 us
    ppermute x21, waiting for transfers between devices: 50 us -> 45.2 us  [swap(): return lax.ppermute(array, axis, [(i, i ^ mask) for i in range(size)])]
    ppermute x21, starting transfers between devices: 23.9 us -> 28.1 us  [swap(): return lax.ppermute(array, axis, [(i, i ^ mask) for i in range(size)])]
  transfers between devices with their start and end apart: 21 -> 21, of which waited for: 13 -> 11; matrix products, arithmetic and copies ran while one was open for 5% -> 5% of each run, Pallas kernels for 38% -> 39%
where the time goes in v2:
time: 139 us; the launch traced here: 138 us
  Pallas kernels  54.8 us (39%)
  waiting for transfers between devices  45.2 us (33%)
  starting transfers between devices  28.1 us (20%)
  local copies, waits for them, and re-layouts  8.37 us (6%)
    ppermute x21, waiting for transfers between devices, swap(): return lax.ppermute(array, axis, [(i, i ^ mask) for i in range(size)])  45.2 us
    pallas_call x8, Pallas kernels, attend(): pl.pallas_call(functools.partial(attend_kernel, settings), out_shape=out_...  37.3 us
    ppermute x21, starting transfers between devices, swap(): return lax.ppermute(array, axis, [(i, i ^ mask) for i in range(size)])  28.1 us
    pallas_call x2, Pallas kernels, pack(): pl.pallas_call(functools.partial(pack_kernel, wanted, per_peer), out_shap...  10.9 us
    pallas_call x4, Pallas kernels, project(): pl.pallas_call(project_kernel, out_shape=[jax.ShapeDtypeStruct((2, share,...  3.16 us
    unnamed x28, local copies, waits for them, and re-layouts  3.12 us
  transfers between devices with their start and end apart: 21, of which 11 were waited for; matrix products, arithmetic and copies ran while one was open for 5% of the time, Pallas kernels for 39%

profile of v2, /device:TPU:0, one launch (start us, length us, event | category | flops | bytes accessed | tf_op | source)
XLA Modules:
  0.0 138.1 jit_solution(2084322694768378616)
XLA Ops:
  0.0 4.0 %collective-permute-start = (bf16[2048,128]{1,0:T(8,128)(2,1)}, bf16[2048,128]{1,0:T(8,128)(2,1)S(1)}, u32[]{:S(2)}, u32[]{:S(2)}) collective-permute-start(bf16[2048,128]{1,0:T(8,128)(2,1)} %bitcast.14), channel_id=1, source_target_pairs={{0,8},{2,10},{4,12},{6,14},{8,0},{10,2},{12,4},{14,6},{1,9},{3,11}... | collective-permute-start | bytes 1572872 | tf_op jit(solution)/shard_map/ppermute | solution.py:20
  4.0 4.7 %pack_pieces.2 = (bf16[8,2,128,128]{3,2,1,0:T(8,128)(2,1)}, bf16[8,2,128,128]{3,2,1,0:T(8,128)(2,1)}, bf16[8,2,128,128]{3,2,1,0:T(8,128)(2,1)}) custom-call(s32[16,32]{1,0:T(8,128)} %slot_ref.3, s32[2,8]{1,0:T(2,128)} %bitcast.21, bf16[64,1,2,128,128]{4,3,2,1,0:T(8,128)(2,1)} %kv_ref.2), custom_call_target="tpu_custom_call" | custom-call | flops 1024 | bytes 1024 | tf_op jit(solution)/shard_map/pack_pieces/pallas_call | solution.py:66
  8.8 1.6 %collective-permute-start.1 = (bf16[8,2,128,128]{3,2,1,0:T(8,128)(2,1)}, bf16[8,2,128,128]{3,2,1,0:T(8,128)(2,1)S(1)}, u32[]{:S(2)}, u32[]{:S(2)}) collective-permute-start(bf16[8,2,128,128]{3,2,1,0:T(8,128)(2,1)} %get-tuple-element.55), channel_id=1, source_target_pairs={{0,2},{2,0},{4,6},{6,4},{8,10},{10,8},{12,14},{14,12},{1,3},{3,1},... | collective-permute-start | bytes 1572872 | tf_op jit(solution)/shard_map/ppermute | solution.py:20
  10.4 1.6 %collective-permute-start.6 = (bf16[8,2,128,128]{3,2,1,0:T(8,128)(2,1)}, bf16[8,2,128,128]{3,2,1,0:T(8,128)(2,1)S(1)}, u32[]{:S(2)}, u32[]{:S(2)}) collective-permute-start(bf16[8,2,128,128]{3,2,1,0:T(8,128)(2,1)} %get-tuple-element.56), channel_id=1, source_target_pairs={{0,4},{2,6},{4,0},{6,2},{8,12},{10,14},{12,8},{14,10},{1,5},{3,7},... | collective-permute-start | bytes 1572872 | tf_op jit(solution)/shard_map/ppermute | solution.py:20
  11.9 0.4 collective-permute-start.5
  12.4 0.2 dynamic-slice_reduce_fusion
  12.6 0.6 gather_fusion
  13.2 0.6 gather_fusion.3
  13.8 0.6 gather_fusion.2
  14.4 0.6 gather_fusion.5
  15.0 0.5 convert_reduce_fusion
  15.5 0.6 gather_fusion.4
  16.3 6.2 %pack_pieces.3 = (bf16[8,2,128,128]{3,2,1,0:T(8,128)(2,1)}, bf16[8,2,128,128]{3,2,1,0:T(8,128)(2,1)}, bf16[8,2,128,128]{3,2,1,0:T(8,128)(2,1)}, bf16[8,2,128,128]{3,2,1,0:T(8,128)(2,1)}, bf16[8,2,128,128]{3,2,1,0:T(8,128)(2,1)}) custom-call(s32[16,32]{1,0:T(8,128)} %slot_ref.3, s32[2,8]{1,0:T(2,128)} %bitcast.22, bf16[64,1,2,128,128]{4,3,2,1,0:T(8,128)(2,1)} %kv_ref.2), custom_call_target="tpu_custom_call" | custom-call | flops 1024 | bytes 1024 | tf_op jit(solution)/shard_map/pack_pieces/pallas_call | solution.py:66
  22.5 0.6 gather_fusion.1
  23.0 0.2 select_reduce_fusion
  23.3 0.1 reshape.176.refs_1_
  23.4 0.2 select_reduce_fusion.1
  23.6 0.1 reshape.175.refs_1_
  23.7 1.0 copy-done.5
  24.7 5.3 %attend_own_local.1 = (f32[2048,128]{1,0:T(8,128)S(1)}, f32[4,4,128]{2,1,0:T(4,128)S(1)}) custom-call(bf16[2048,128]{1,0:T(8,128)(2,1)S(1)} %bitcast.15, s32[4,8]{1,0:T(4,128)S(1)} %reshape.175.refs_1_, bf16[128,128]{1,0:T(8,128)(2,1)S(1)} %bitcast.19, bf16[128,128]{1,0:T(8,128)(2,1)S(1)} %bitcast.20, bf16[8,2,128,128]{3,2,1,0:T(8,128)(2,1)S(1)} %copy-done.5), custom_call_target="tpu_custom_call" | custom-call | flops 1024 | bytes 1024 | tf_op jit(solution)/shard_map/attend_own_local/pallas_call | solution.py:232
  30.1 1.0 copy-done.8
  31.1 4.1 %attend_partner_local.1 = (f32[2048,128]{1,0:T(8,128)S(1)}, f32[4,4,128]{2,1,0:T(4,128)S(1)}) custom-call(bf16[2048,128]{1,0:T(8,128)(2,1)S(1)} %collective-permute-done.refs_0_, s32[4,8]{1,0:T(4,128)S(1)} %reshape.176.refs_1_, bf16[8,2,128,128]{3,2,1,0:T(8,128)(2,1)S(1)} %copy-done.8), custom_call_target="tpu_custom_call" | custom-call | flops 2147483648 | bytes 1024 | tf_op jit(solution)/shard_map/attend_partner_local/pallas_call | solution.py:232
  35.3 4.6 %attend_partner_early.1 = (f32[2048,128]{1,0:T(8,128)S(1)}, f32[4,4,128]{2,1,0:T(4,128)S(1)}) custom-call(bf16[2048,128]{1,0:T(8,128)(2,1)S(1)} %collective-permute-done.refs_0_, s32[4,8]{1,0:T(4,128)S(1)} %reshape.176.refs_1_, bf16[8,2,128,128]{3,2,1,0:T(8,128)(2,1)S(1)} %collective-permute-done.1.refs_2_, f32[2048,128]{1,0:T(8,128)S(1)} %get-tuple-element.66.refs_3_, ...), custom_call_target="tpu_custom_call" | custom-call | flops 1024 | bytes 1024 | tf_op jit(solution)/shard_map/attend_partner_early/pallas_call | solution.py:232
  39.8 1.6 %collective-permute-start.4 = (bf16[8,2,128,128]{3,2,1,0:T(8,128)(2,1)S(1)}, bf16[8,2,128,128]{3,2,1,0:T(8,128)(2,1)S(1)}, u32[]{:S(2)}, u32[]{:S(2)}) collective-permute-start(bf16[8,2,128,128]{3,2,1,0:T(8,128)(2,1)S(1)} %copy-done.13), channel_id=1, source_target_pairs={{0,2},{2,0},{4,6},{6,4},{8,10},{10,8},{12,14},{14,12},{1,3},{3,1},... | collective-permute-start | bytes 1572872 | tf_op jit(solution)/shard_map/ppermute | solution.py:20
  41.4 1.6 %collective-permute-start.3 = (bf16[8,2,128,128]{3,2,1,0:T(8,128)(2,1)S(1)}, bf16[8,2,128,128]{3,2,1,0:T(8,128)(2,1)S(1)}, u32[]{:S(2)}, u32[]{:S(2)}) collective-permute-start(bf16[8,2,128,128]{3,2,1,0:T(8,128)(2,1)S(1)} %copy-done.12), channel_id=1, source_target_pairs={{0,4},{2,6},{4,0},{6,2},{8,12},{10,14},{12,8},{14,10},{1,5},{3,7},... | collective-permute-start | bytes 1572872 | tf_op jit(solution)/shard_map/ppermute | solution.py:20
  43.0 0.4 collective-permute-start.2
  43.4 4.6 %attend_partner_late.1 = (f32[2048,128]{1,0:T(8,128)S(1)}, f32[4,4,128]{2,1,0:T(4,128)S(1)}) custom-call(bf16[2048,128]{1,0:T(8,128)(2,1)S(1)} %collective-permute-done.refs_0_, s32[4,8]{1,0:T(4,128)S(1)} %reshape.176.refs_1_, bf16[8,2,128,128]{3,2,1,0:T(8,128)(2,1)S(1)} %collective-permute-done.6.refs_2_, f32[2048,128]{1,0:T(8,128)S(1)} %get-tuple-element.68.refs_3_, ...), custom_call_target="tpu_custom_call" | custom-call | flops 1024 | bytes 1024 | tf_op jit(solution)/shard_map/attend_partner_late/pallas_call | solution.py:232
  48.0 5.1 %attend_partner_last.1 = (bf16[1072,128]{1,0:T(8,128)(2,1)S(1)}, bf16[1024,128]{1,0:T(8,128)(2,1)S(1)}) custom-call(bf16[2048,128]{1,0:T(8,128)(2,1)S(1)} %collective-permute-done.refs_0_, s32[4,8]{1,0:T(4,128)S(1)} %reshape.176.refs_1_, bf16[8,2,128,128]{3,2,1,0:T(8,128)(2,1)S(1)} %collective-permute-done.5.refs_2_, ...), custom_call_target="tpu_custom_call" | custom-call | flops 1024 | bytes 1024 | tf_op jit(solution)/shard_map/attend_partner_last/pallas_call | solution.py:232
  53.1 1.6 %collective-permute-start.7 = (bf16[384,512]{1,0:T(8,128)(2,1)S(1)}, bf16[384,512]{1,0:T(8,128)(2,1)S(1)}, u32[]{:S(2)}, u32[]{:S(2)}) collective-permute-start(bf16[384,512]{1,0:T(8,128)(2,1)S(1)} %slice.6), channel_id=1, source_target_pairs={{0,2},{2,0},{4,6},{6,4},{8,10},{10,8},{12,14},{14,12},{1,3},{3,1},... | collective-permute-start | bytes 1179656 | tf_op jit(solution)/shard_map/ppermute | solution.py:20
  54.7 0.3 collective-permute-start.8
  55.0 2.0 %collective-permute-done.4.refs_2_ = bf16[8,2,128,128]{3,2,1,0:T(8,128)(2,1)S(1)} collective-permute-done((bf16[8,2,128,128]{3,2,1,0:T(8,128)(2,1)S(1)}, bf16[8,2,128,128]{3,2,1,0:T(8,128)(2,1)S(1)}, u32[]{:S(2)}, u32[]{:S(2)}) %collective-permute-start.4) | collective-permute-done | bytes 524320 | tf_op jit(solution)/shard_map/ppermute | solution.py:20
  57.0 0.6 collective-permute-start.9
  57.6 1.3 slice.7
  58.9 4.6 %attend_own_early.1 = (f32[2048,128]{1,0:T(8,128)S(1)}, f32[4,4,128]{2,1,0:T(4,128)S(1)}) custom-call(bf16[2048,128]{1,0:T(8,128)(2,1)S(1)} %bitcast.16, s32[4,8]{1,0:T(4,128)S(1)} %reshape.175.refs_1_, bf16[8,2,128,128]{3,2,1,0:T(8,128)(2,1)S(1)} %collective-permute-done.4.refs_2_, f32[2048,128]{1,0:T(8,128)S(1)} %get-tuple-element.79.refs_3_, ...), custom_call_target="tpu_custom_call" | custom-call | flops 1024 | bytes 1024 | tf_op jit(solution)/shard_map/attend_own_early/pallas_call | solution.py:232
  63.5 2.5 %collective-permute-done.7.w_sooner = bf16[384,512]{1,0:T(8,128)(2,1)S(1)} collective-permute-done((bf16[384,512]{1,0:T(8,128)(2,1)S(1)}, bf16[384,512]{1,0:T(8,128)(2,1)S(1)}, u32[]{:S(2)}, u32[]{:S(2)}) %collective-permute-start.7) | collective-permute-done | bytes 393248 | tf_op jit(solution)/shard_map/ppermute | solution.py:20
  66.0 1.2 collective-permute-done.3.refs_2_
  67.2 4.6 %attend_own_late.1 = (f32[2048,128]{1,0:T(8,128)S(1)}, f32[4,4,128]{2,1,0:T(4,128)S(1)}) custom-call(bf16[2048,128]{1,0:T(8,128)(2,1)S(1)} %bitcast.17, s32[4,8]{1,0:T(4,128)S(1)} %reshape.175.refs_1_, bf16[8,2,128,128]{3,2,1,0:T(8,128)(2,1)S(1)} %collective-permute-done.3.refs_2_, f32[2048,128]{1,0:T(8,128)S(1)} %get-tuple-element.84.refs_3_, ...), custom_call_target="tpu_custom_call" | custom-call | flops 1024 | bytes 1024 | tf_op jit(solution)/shard_map/attend_own_late/pallas_call | solution.py:232
  71.8 0.8 collective-permute-start.12
  72.6 4.4 %collective-permute-done.2.refs_2_ = bf16[8,2,128,128]{3,2,1,0:T(8,128)(2,1)S(1)} collective-permute-done((bf16[8,2,128,128]{3,2,1,0:T(8,128)(2,1)S(1)}, bf16[8,2,128,128]{3,2,1,0:T(8,128)(2,1)S(1)}, u32[]{:S(2)}, u32[]{:S(2)}) %collective-permute-start.2) | collective-permute-done | bytes 524320 | tf_op jit(solution)/shard_map/ppermute | solution.py:20
  77.0 4.6 %attend_own_last.1 = (f32[2048,128]{1,0:T(8,128)S(1)}, f32[4,4,128]{2,1,0:T(4,128)S(1)}) custom-call(bf16[2048,128]{1,0:T(8,128)(2,1)S(1)} %bitcast.18, s32[4,8]{1,0:T(4,128)S(1)} %reshape.175.refs_1_, bf16[8,2,128,128]{3,2,1,0:T(8,128)(2,1)S(1)} %collective-permute-done.2.refs_2_, f32[2048,128]{1,0:T(8,128)S(1)} %get-tuple-element.86.refs_3_, ...), custom_call_target="tpu_custom_call" | custom-call | flops 1024 | bytes 1024 | tf_op jit(solution)/shard_map/attend_own_last/pallas_call | solution.py:232
  81.5 0.6 combine.1.attended
  82.1 2.7 %collective-permute-start.10 = (bf16[128,2048]{1,0:T(8,128)(2,1)S(1)}, bf16[128,2048]{1,0:T(8,128)(2,1)S(1)}, u32[]{:S(2)}, u32[]{:S(2)}) collective-permute-start(bf16[128,2048]{1,0:T(8,128)(2,1)S(1)} %combine.1.attended), channel_id=1, source_target_pairs={{0,8},{2,10},{4,12},{6,14},{8,0},{10,2},{12,4},{14,6},{1,9},{3,11}... | collective-permute-start | bytes 1572872 | tf_op jit(solution)/shard_map/ppermute | solution.py:20
  84.8 2.5 %collective-permute-start.11 = (bf16[128,2048]{1,0:T(8,128)(2,1)S(1)}, bf16[128,2048]{1,0:T(8,128)(2,1)S(1)}, u32[]{:S(2)}, u32[]{:S(2)}) collective-permute-start(bf16[128,2048]{1,0:T(8,128)(2,1)S(1)} %combine.1.attended), channel_id=1, source_target_pairs={{0,4},{2,6},{4,0},{6,2},{8,12},{10,14},{12,8},{14,10},{1,5},{3,7},... | collective-permute-start | bytes 1572872 | tf_op jit(solution)/shard_map/ppermute | solution.py:20
  87.3 19.6 %collective-permute-done.10.attended = bf16[128,2048]{1,0:T(8,128)(2,1)S(1)} collective-permute-done((bf16[128,2048]{1,0:T(8,128)(2,1)S(1)}, bf16[128,2048]{1,0:T(8,128)(2,1)S(1)}, u32[]{:S(2)}, u32[]{:S(2)}) %collective-permute-start.10) | collective-permute-done | bytes 524320 | tf_op jit(solution)/shard_map/ppermute | solution.py:20
  106.9 1.8 %collective-permute-start.18 = (bf16[128,2048]{1,0:T(8,128)(2,1)S(1)}, bf16[128,2048]{1,0:T(8,128)(2,1)S(1)}, u32[]{:S(2)}, u32[]{:S(2)}) collective-permute-start(bf16[128,2048]{1,0:T(8,128)(2,1)S(1)} %collective-permute-done.10.attended), channel_id=1, source_target_pairs={{0,4},{2,6},{4,0},{6,2},{8,12},{10,14},{12,8},{14,10},{1,5},{3,7},... | collective-permute-start | bytes 1572872 | tf_op jit(solution)/shard_map/ppermute | solution.py:20
  108.7 0.4 stage.2.w_mine
  109.1 4.3 %collective-permute-done.12.source = bf16[1664,512]{1,0:T(8,128)(2,1)} collective-permute-done((bf16[1664,512]{1,0:T(8,128)(2,1)}, bf16[1664,512]{1,0:T(8,128)(2,1)}, u32[]{:S(2)}, u32[]{:S(2)}) %collective-permute-start.12) | collective-permute-done | bytes 1703968 | tf_op jit(solution)/shard_map/ppermute | solution.py:20
  113.5 1.6 %stage.3.w_later = bf16[1664,512]{1,0:T(8,128)(2,1)S(1)} custom-call(bf16[1664,512]{1,0:T(8,128)(2,1)} %collective-permute-done.12.source), custom_call_target="tpu_custom_call" | custom-call | flops 1024 | bytes 1024 | tf_op jit(solution)/shard_map/stage/pallas_call | solution.py:296
  115.1 0.8 project.6
  115.9 1.0 copy-done.4
  116.9 0.8 project.5
  117.7 0.8 project.4
  118.5 0.3 collective-permute-done.18.attended
  118.7 0.8 project.7
  119.6 0.5 collective-permute-start.17
  120.1 0.1 collective-permute-start.15
  120.2 0.4 collective-permute-start.13
  120.6 0.3 collective-permute-done.19
  121.0 4.5 %collective-permute-start.20 = (bf16[2,64,512]{2,1,0:T(8,128)(2,1)S(1)}, bf16[2,64,512]{2,1,0:T(8,128)(2,1)S(1)}, u32[]{:S(2)}, u32[]{:S(2)}) collective-permute-start(bf16[2,64,512]{2,1,0:T(8,128)(2,1)S(1)} %add_convert_fusion), channel_id=1, source_target_pairs={{0,12},{2,14},{4,8},{6,10},{8,4},{10,6},{12,0},{14,2},{1,13},{3,15... | collective-permute-start | bytes 393224 | tf_op jit(solution)/shard_map/ppermute | solution.py:20
  125.6 1.0 collective-permute-start.14
  126.7 3.1 %collective-permute-done.20.refs_3_ = bf16[2,64,512]{2,1,0:T(8,128)(2,1)S(1)} collective-permute-done((bf16[2,64,512]{2,1,0:T(8,128)(2,1)S(1)}, bf16[2,64,512]{2,1,0:T(8,128)(2,1)S(1)}, u32[]{:S(2)}, u32[]{:S(2)}) %collective-permute-start.20) | collective-permute-done | bytes 131104 | tf_op jit(solution)/shard_map/ppermute | solution.py:20
  129.8 3.0 %collective-permute-done.16.refs_1_ = bf16[2,64,512]{2,1,0:T(8,128)(2,1)S(1)} collective-permute-done((bf16[2,64,512]{2,1,0:T(8,128)(2,1)S(1)}, bf16[2,64,512]{2,1,0:T(8,128)(2,1)S(1)}, u32[]{:S(2)}, u32[]{:S(2)}) %collective-permute-start.16) | collective-permute-done | bytes 131104 | tf_op jit(solution)/shard_map/ppermute | solution.py:20
  132.8 4.5 %collective-permute-done.14.refs_0_ = bf16[2,64,512]{2,1,0:T(8,128)(2,1)S(1)} collective-permute-done((bf16[2,64,512]{2,1,0:T(8,128)(2,1)S(1)}, bf16[2,64,512]{2,1,0:T(8,128)(2,1)S(1)}, u32[]{:S(2)}, u32[]{:S(2)}) %collective-permute-start.14) | collective-permute-done | bytes 131104 | tf_op jit(solution)/shard_map/ppermute | solution.py:20
  137.2 0.8 place_columns.1
  (53 shorter events, 0.6 us)
Async XLA Ops:
  0.0 13.7 %copy-start = (s32[16]{0:T(128)S(1)}, s32[16]{0:T(128)}, u32[]{:S(2)}) copy-start(s32[16]{0:T(128)} %param.12) | copy-start | bytes 196
  0.0 30.1 %collective-permute-start = (bf16[2048,128]{1,0:T(8,128)(2,1)}, bf16[2048,128]{1,0:T(8,128)(2,1)S(1)}, u32[]{:S(2)}, u32[]{:S(2)}) collective-permute-start(bf16[2048,128]{1,0:T(8,128)(2,1)} %bitcast.14), channel_id=1, source_target_pairs={{0,8},{2,10},{4,12},{6,14},{8,0},{10,2},{12,4},{14,6},{1,9},{3,11}... | collective-permute-start | bytes 1572872 | tf_op jit(solution)/shard_map/ppermute | solution.py:20
  4.0 8.3 %copy-start.9 = (s32[16,32]{1,0:T(8,128)S(1)}, s32[16,32]{1,0:T(8,128)}, u32[]{:S(2)}) copy-start(s32[16,32]{1,0:T(8,128)} %slot_ref.3) | copy-start | bytes 6148
  4.0 8.3 %copy-start.10 = (s32[8,1,2]{0,2,1:T(2,128)S(1)}, s32[8,1,2]{0,2,1:T(2,128)}, u32[]{:S(2)}) copy-start(s32[8,1,2]{0,2,1:T(2,128)} %param.14) | copy-start | bytes 196
  8.8 26.5 %collective-permute-start.1 = (bf16[8,2,128,128]{3,2,1,0:T(8,128)(2,1)}, bf16[8,2,128,128]{3,2,1,0:T(8,128)(2,1)S(1)}, u32[]{:S(2)}, u32[]{:S(2)}) collective-permute-start(bf16[8,2,128,128]{3,2,1,0:T(8,128)(2,1)} %get-tuple-element.55), channel_id=1, source_target_pairs={{0,2},{2,0},{4,6},{6,4},{8,10},{10,8},{12,14},{14,12},{1,3},{3,1},... | collective-permute-start | bytes 1572872 | tf_op jit(solution)/shard_map/ppermute | solution.py:20
  10.4 33.1 %collective-permute-start.6 = (bf16[8,2,128,128]{3,2,1,0:T(8,128)(2,1)}, bf16[8,2,128,128]{3,2,1,0:T(8,128)(2,1)S(1)}, u32[]{:S(2)}, u32[]{:S(2)}) collective-permute-start(bf16[8,2,128,128]{3,2,1,0:T(8,128)(2,1)} %get-tuple-element.56), channel_id=1, source_target_pairs={{0,4},{2,6},{4,0},{6,2},{8,12},{10,14},{12,8},{14,10},{1,5},{3,7},... | collective-permute-start | bytes 1572872 | tf_op jit(solution)/shard_map/ppermute | solution.py:20
  11.9 36.1 %collective-permute-start.5 = (bf16[8,2,128,128]{3,2,1,0:T(8,128)(2,1)}, bf16[8,2,128,128]{3,2,1,0:T(8,128)(2,1)S(1)}, u32[]{:S(2)}, u32[]{:S(2)}) collective-permute-start(bf16[8,2,128,128]{3,2,1,0:T(8,128)(2,1)} %get-tuple-element.57), channel_id=1, source_target_pairs={{0,6},{2,4},{4,2},{6,0},{8,14},{10,12},{12,10},{14,8},{1,7},{3,5},... | collective-permute-start | bytes 1572872 | tf_op jit(solution)/shard_map/ppermute | solution.py:20
  16.2 7.4 %copy-start.1 = (bf16[128,16,128]{2,1,0:T(8,128)(2,1)S(1)}, bf16[128,16,128]{2,1,0:T(8,128)(2,1)}, u32[]{:S(2)}) copy-start(bf16[128,16,128]{2,1,0:T(8,128)(2,1)} %param.8) | copy-start | bytes 1572868
  16.2 7.4 %copy-start.6 = (bf16[128,1,128]{2,0,1:T(8,128)(2,1)S(1)}, bf16[128,1,128]{2,0,1:T(8,128)(2,1)}, u32[]{:S(2)}) copy-start(bf16[128,1,128]{2,0,1:T(8,128)(2,1)} %param.9) | copy-start | bytes 98308
  16.3 7.4 %copy-start.7 = (bf16[128,1,128]{2,0,1:T(8,128)(2,1)S(1)}, bf16[128,1,128]{2,0,1:T(8,128)(2,1)}, u32[]{:S(2)}) copy-start(bf16[128,1,128]{2,0,1:T(8,128)(2,1)} %param.10) | copy-start | bytes 98308
  23.7 1.0 copy-start.5
  30.1 1.0 copy-start.8
  31.1 8.7 %copy-start.13 = (bf16[8,2,128,128]{3,2,1,0:T(8,128)(2,1)S(1)}, bf16[8,2,128,128]{3,2,1,0:T(8,128)(2,1)}, u32[]{:S(2)}) copy-start(bf16[8,2,128,128]{3,2,1,0:T(8,128)(2,1)} %get-tuple-element.74) | copy-start | bytes 1572868
  31.1 10.3 %copy-start.12 = (bf16[8,2,128,128]{3,2,1,0:T(8,128)(2,1)S(1)}, bf16[8,2,128,128]{3,2,1,0:T(8,128)(2,1)}, u32[]{:S(2)}) copy-start(bf16[8,2,128,128]{3,2,1,0:T(8,128)(2,1)} %get-tuple-element.72) | copy-start | bytes 1572868
  31.1 11.9 %copy-start.11 = (bf16[8,2,128,128]{3,2,1,0:T(8,128)(2,1)S(1)}, bf16[8,2,128,128]{3,2,1,0:T(8,128)(2,1)}, u32[]{:S(2)}) copy-start(bf16[8,2,128,128]{3,2,1,0:T(8,128)(2,1)} %get-tuple-element.70) | copy-start | bytes 1572868
  35.2 8.2 %copy-start.2 = (bf16[2048,512]{1,0:T(8,128)(2,1)S(1)}, bf16[2048,512]{1,0:T(8,128)(2,1)}, u32[]{:S(2)}) copy-start(bf16[2048,512]{1,0:T(8,128)(2,1)} %source) | copy-start | bytes 6291460
  39.8 17.2 %collective-permute-start.4 = (bf16[8,2,128,128]{3,2,1,0:T(8,128)(2,1)S(1)}, bf16[8,2,128,128]{3,2,1,0:T(8,128)(2,1)S(1)}, u32[]{:S(2)}, u32[]{:S(2)}) collective-permute-start(bf16[8,2,128,128]{3,2,1,0:T(8,128)(2,1)S(1)} %copy-done.13), channel_id=1, source_target_pairs={{0,2},{2,0},{4,6},{6,4},{8,10},{10,8},{12,14},{14,12},{1,3},{3,1},... | collective-permute-start | bytes 1572872 | tf_op jit(solution)/shard_map/ppermute | solution.py:20
  41.4 25.8 %collective-permute-start.3 = (bf16[8,2,128,128]{3,2,1,0:T(8,128)(2,1)S(1)}, bf16[8,2,128,128]{3,2,1,0:T(8,128)(2,1)S(1)}, u32[]{:S(2)}, u32[]{:S(2)}) collective-permute-start(bf16[8,2,128,128]{3,2,1,0:T(8,128)(2,1)S(1)} %copy-done.12), channel_id=1, source_target_pairs={{0,4},{2,6},{4,0},{6,2},{8,12},{10,14},{12,8},{14,10},{1,5},{3,7},... | collective-permute-start | bytes 1572872 | tf_op jit(solution)/shard_map/ppermute | solution.py:20
  43.0 33.9 %collective-permute-start.2 = (bf16[8,2,128,128]{3,2,1,0:T(8,128)(2,1)S(1)}, bf16[8,2,128,128]{3,2,1,0:T(8,128)(2,1)S(1)}, u32[]{:S(2)}, u32[]{:S(2)}) collective-permute-start(bf16[8,2,128,128]{3,2,1,0:T(8,128)(2,1)S(1)} %copy-done.11), channel_id=1, source_target_pairs={{0,6},{2,4},{4,2},{6,0},{8,14},{10,12},{12,10},{14,8},{1,7},{3,5},... | collective-permute-start | bytes 1572872 | tf_op jit(solution)/shard_map/ppermute | solution.py:20
  53.1 12.9 %collective-permute-start.7 = (bf16[384,512]{1,0:T(8,128)(2,1)S(1)}, bf16[384,512]{1,0:T(8,128)(2,1)S(1)}, u32[]{:S(2)}, u32[]{:S(2)}) collective-permute-start(bf16[384,512]{1,0:T(8,128)(2,1)S(1)} %slice.6), channel_id=1, source_target_pairs={{0,2},{2,0},{4,6},{6,4},{8,10},{10,8},{12,14},{14,12},{1,3},{3,1},... | collective-permute-start | bytes 1179656 | tf_op jit(solution)/shard_map/ppermute | solution.py:20
  54.7 26.9 %collective-permute-start.8 = (bf16[1072,128]{1,0:T(8,128)(2,1)S(1)}, bf16[1072,128]{1,0:T(8,128)(2,1)S(1)}, u32[]{:S(2)}, u32[]{:S(2)}) collective-permute-start(bf16[1072,128]{1,0:T(8,128)(2,1)S(1)} %get-tuple-element.77), channel_id=1, source_target_pairs={{0,8},{2,10},{4,12},{6,14},{8,0},{10,2},{12,4},{14,6},{1,9},{3,11}... | collective-permute-start | bytes 823304 | tf_op jit(solution)/shard_map/ppermute | solution.py:20
  57.0 24.5 %collective-permute-start.9 = (bf16[1024,128]{1,0:T(8,128)(2,1)S(1)}, bf16[1024,128]{1,0:T(8,128)(2,1)S(1)}, u32[]{:S(2)}, u32[]{:S(2)}) collective-permute-start(bf16[1024,128]{1,0:T(8,128)(2,1)S(1)} %get-tuple-element.78), channel_id=1, source_target_pairs={{0,8},{2,10},{4,12},{6,14},{8,0},{10,2},{12,4},{14,6},{1,9},{3,11}... | collective-permute-start | bytes 786440 | tf_op jit(solution)/shard_map/ppermute | solution.py:20
  66.0 49.0 %copy-start.3 = (bf16[384,512]{1,0:T(8,128)(2,1)}, bf16[384,512]{1,0:T(8,128)(2,1)S(1)}, u32[]{:S(2)}) copy-start(bf16[384,512]{1,0:T(8,128)(2,1)S(1)} %collective-permute-done.7.w_sooner) | copy-start | bytes 1179652
  71.8 41.7 %collective-permute-start.12 = (bf16[1664,512]{1,0:T(8,128)(2,1)}, bf16[1664,512]{1,0:T(8,128)(2,1)}, u32[]{:S(2)}, u32[]{:S(2)}) collective-permute-start(bf16[1664,512]{1,0:T(8,128)(2,1)} %slice.7), channel_id=1, source_target_pairs={{0,2},{2,0},{4,6},{6,4},{8,10},{10,8},{12,14},{14,12},{1,3},{3,1},... | collective-permute-start | bytes 5111816 | tf_op jit(solution)/shard_map/ppermute | solution.py:20
  82.1 24.8 %collective-permute-start.10 = (bf16[128,2048]{1,0:T(8,128)(2,1)S(1)}, bf16[128,2048]{1,0:T(8,128)(2,1)S(1)}, u32[]{:S(2)}, u32[]{:S(2)}) collective-permute-start(bf16[128,2048]{1,0:T(8,128)(2,1)S(1)} %combine.1.attended), channel_id=1, source_target_pairs={{0,8},{2,10},{4,12},{6,14},{8,0},{10,2},{12,4},{14,6},{1,9},{3,11}... | collective-permute-start | bytes 1572872 | tf_op jit(solution)/shard_map/ppermute | solution.py:20
  84.8 22.1 %collective-permute-start.11 = (bf16[128,2048]{1,0:T(8,128)(2,1)S(1)}, bf16[128,2048]{1,0:T(8,128)(2,1)S(1)}, u32[]{:S(2)}, u32[]{:S(2)}) collective-permute-start(bf16[128,2048]{1,0:T(8,128)(2,1)S(1)} %combine.1.attended), channel_id=1, source_target_pairs={{0,4},{2,6},{4,0},{6,2},{8,12},{10,14},{12,8},{14,10},{1,5},{3,7},... | collective-permute-start | bytes 1572872 | tf_op jit(solution)/shard_map/ppermute | solution.py:20
  106.9 11.8 %collective-permute-start.18 = (bf16[128,2048]{1,0:T(8,128)(2,1)S(1)}, bf16[128,2048]{1,0:T(8,128)(2,1)S(1)}, u32[]{:S(2)}, u32[]{:S(2)}) collective-permute-start(bf16[128,2048]{1,0:T(8,128)(2,1)S(1)} %collective-permute-done.10.attended), channel_id=1, source_target_pairs={{0,4},{2,6},{4,0},{6,2},{8,12},{10,14},{12,8},{14,10},{1,5},{3,7},... | collective-permute-start | bytes 1572872 | tf_op jit(solution)/shard_map/ppermute | solution.py:20
  115.9 1.0 copy-start.4
  119.5 1.4 %collective-permute-start.19 = (bf16[2,64,512]{2,1,0:T(8,128)(2,1)S(1)}, bf16[2,64,512]{2,1,0:T(8,128)(2,1)S(1)}, u32[]{:S(2)}, u32[]{:S(2)}) collective-permute-start(bf16[2,64,512]{2,1,0:T(8,128)(2,1)S(1)} %get-tuple-element.104), channel_id=1, source_target_pairs={{0,1},{1,0},{2,3},{3,2},{4,5},{5,4},{6,7},{7,6},{8,9},{9,8},{10,11... | collective-permute-start | bytes 393224 | tf_op jit(solution)/shard_map/ppermute | solution.py:20
  119.6 7.0 %collective-permute-start.17 = (bf16[2,64,512]{2,1,0:T(8,128)(2,1)S(1)}, bf16[2,64,512]{2,1,0:T(8,128)(2,1)S(1)}, u32[]{:S(2)}, u32[]{:S(2)}) collective-permute-start(bf16[2,64,512]{2,1,0:T(8,128)(2,1)S(1)} %get-tuple-element.100), channel_id=1, source_target_pairs={{0,1},{1,0},{2,3},{3,2},{4,5},{5,4},{6,7},{7,6},{8,9},{9,8},{10,11... | collective-permute-start | bytes 393224 | tf_op jit(solution)/shard_map/ppermute | solution.py:20
  120.1 5.4 %collective-permute-start.15 = (bf16[2,64,512]{2,1,0:T(8,128)(2,1)S(1)}, bf16[2,64,512]{2,1,0:T(8,128)(2,1)S(1)}, u32[]{:S(2)}, u32[]{:S(2)}) collective-permute-start(bf16[2,64,512]{2,1,0:T(8,128)(2,1)S(1)} %get-tuple-element.97), channel_id=1, source_target_pairs={{0,1},{1,0},{2,3},{3,2},{4,5},{5,4},{6,7},{7,6},{8,9},{9,8},{10,11... | collective-permute-start | bytes 393224 | tf_op jit(solution)/shard_map/ppermute | solution.py:20
  120.2 5.4 %collective-permute-start.13 = (bf16[2,64,512]{2,1,0:T(8,128)(2,1)S(1)}, bf16[2,64,512]{2,1,0:T(8,128)(2,1)S(1)}, u32[]{:S(2)}, u32[]{:S(2)}) collective-permute-start(bf16[2,64,512]{2,1,0:T(8,128)(2,1)S(1)} %get-tuple-element.94), channel_id=1, source_target_pairs={{0,1},{1,0},{2,3},{3,2},{4,5},{5,4},{6,7},{7,6},{8,9},{9,8},{10,11... | collective-permute-start | bytes 393224 | tf_op jit(solution)/shard_map/ppermute | solution.py:20
  121.0 8.8 %collective-permute-start.20 = (bf16[2,64,512]{2,1,0:T(8,128)(2,1)S(1)}, bf16[2,64,512]{2,1,0:T(8,128)(2,1)S(1)}, u32[]{:S(2)}, u32[]{:S(2)}) collective-permute-start(bf16[2,64,512]{2,1,0:T(8,128)(2,1)S(1)} %add_convert_fusion), channel_id=1, source_target_pairs={{0,12},{2,14},{4,8},{6,10},{8,4},{10,6},{12,0},{14,2},{1,13},{3,15... | collective-permute-start | bytes 393224 | tf_op jit(solution)/shard_map/ppermute | solution.py:20
  125.5 7.2 %collective-permute-start.16 = (bf16[2,64,512]{2,1,0:T(8,128)(2,1)S(1)}, bf16[2,64,512]{2,1,0:T(8,128)(2,1)S(1)}, u32[]{:S(2)}, u32[]{:S(2)}) collective-permute-start(bf16[2,64,512]{2,1,0:T(8,128)(2,1)S(1)} %add_convert_fusion.2), channel_id=1, source_target_pairs={{0,4},{2,6},{4,0},{6,2},{8,12},{10,14},{12,8},{14,10},{1,5},{3,7},... | collective-permute-start | bytes 393224 | tf_op jit(solution)/shard_map/ppermute | solution.py:20
  125.6 11.6 %collective-permute-start.14 = (bf16[2,64,512]{2,1,0:T(8,128)(2,1)S(1)}, bf16[2,64,512]{2,1,0:T(8,128)(2,1)S(1)}, u32[]{:S(2)}, u32[]{:S(2)}) collective-permute-start(bf16[2,64,512]{2,1,0:T(8,128)(2,1)S(1)} %add_convert_fusion.3), channel_id=1, source_target_pairs={{0,8},{2,10},{4,12},{6,14},{8,0},{10,2},{12,4},{14,6},{1,9},{3,11}... | collective-permute-start | bytes 393224 | tf_op jit(solution)/shard_map/ppermute | solution.py:20
